TPU v7x, 32 devices: a whole 2x2x4 slice. The times are simulated.
32 devices in a mesh: groups: 2 (over y), shard: 8 (over z, x), rep: 2 (over core).
Axes of the slice: x: 2, y: 2, z: 4, core: 2. Of those that a mesh axis runs over, the one named last changes fastest.
Arguments:
- queries: bfloat16 [256, 32, 128], P(('groups', 'shard', 'rep')), parts along dimension 0, may hold values from -1.796875 to 1.796875
- passages: bfloat16 [1024, 192, 128], P(('groups', 'shard')), parts along dimension 0, may hold values from -1.796875 to 1.796875
- lengths: int32 [1024], P(('groups', 'shard')), parts along dimension 0, may hold values from 24 to 192
- token_mask: int32 [1024, 192], P(('groups', 'shard')), parts along dimension 0, may hold values 0 or 1
- cand_owner: int32 [256, 100], P(('groups', 'shard', 'rep')), parts along dimension 0, may hold values from 0 to 7, as said below
- cand_slot: int32 [256, 100], P(('groups', 'shard', 'rep')), parts along dimension 0, may hold values from 0 to 63
Outputs:
- scores: float32 [256, 100], P(('groups', 'shard', 'rep')), parts along dimension 0
There are 2 independent parts, one for each index of `groups`. A program takes and returns all parts, laid end to end along the dimension named above; each array names one. Nothing has to cross between parts.
Inputs may be any that keep to these rules, and one draw needn't show every extreme that they name: `cand_owner`: no query names more than 13 candidates of one owner, and some query names exactly 13.
All inputs are finite; a program needn't handle non-finite values. No bound on the sum of `token_mask` on one device may be relied on, other than what follows from the above.
Results may differ from a plain program's by a relative error of at most 0.0003.
Values may be sent and summed in bfloat16 or wider, within the bound.
No kernel may reach another device: no remote copies, remote signals or barrier semaphores. Data moves between devices by JAX's collectives and lax.ppermute only.
A program may use at most 64 MiB of HBM per device.

v0:
```python
import jax
import jax.numpy as jnp
from jax import lax
from jax.sharding import PartitionSpec as P


def owner_rank(owners):
    cand_count = owners.shape[1]
    same_owner = owners[:, :, None] == owners[:, None, :]
    earlier = jnp.arange(cand_count)[None, :] < jnp.arange(cand_count)[:, None]
    return jnp.sum(same_owner & earlier[None], axis=2)


def slot_table(owners, slot_ids, rank_in, owner_ids, per_owner):
    is_hit = (owners[:, :, None, None] == owner_ids[None, None, :, None]) & (
        rank_in[:, :, None, None] == jnp.arange(per_owner)[None, None, None, :]
    )
    return jnp.sum(jnp.where(is_hit, slot_ids[:, :, None, None] + 1, 0), axis=1) - 1


def score_pairs(gathered, requests, passages, valid_tok, per_owner):
    row_count = requests.shape[0]
    block_count = 8
    slot_count = passages.shape[0]
    slot_blocks = requests.reshape(block_count, row_count // block_count, per_owner)
    query_blocks = gathered.reshape(
        block_count, row_count // block_count, gathered.shape[1], gathered.shape[2]
    )
    valid_float = valid_tok.astype(jnp.float32)
    slot_range = jnp.arange(slot_count, dtype=jnp.int32)

    def score_block(block_args):
        slot_row, query_tok = block_args
        is_live = slot_row >= 0
        one_hot = slot_row[:, :, None] == slot_range[None, None, :]
        passage_tok = jnp.einsum(
            "bpn,nld->bpld",
            one_hot.astype(passages.dtype),
            passages,
            preferred_element_type=jnp.float32,
        ).astype(jnp.bfloat16)
        keep_mask = jnp.einsum("bpn,nl->bpl", one_hot.astype(jnp.float32), valid_float) > 0.5
        similar = jnp.einsum(
            "btd,bpld->bptl", query_tok, passage_tok, preferred_element_type=jnp.float32
        )
        best_match = jnp.max(jnp.where(keep_mask[:, :, None, :], similar, -1e30), axis=3)
        return jnp.where(is_live, jnp.mean(best_match, axis=2), 0.0)

    return lax.map(score_block, (slot_blocks, query_blocks)).reshape(requests.shape)


def local(queries, passages, lengths, token_mask, cand_owner, cand_slot):
    shard_count = lax.axis_size("shard")
    query_count, cand_count = cand_owner.shape
    per_owner = (cand_count + shard_count - 1) // shard_count
    token_len = passages.shape[1]
    positions = jnp.arange(token_len, dtype=jnp.int32)
    valid_tok = (positions[None, :] < lengths[:, None]) & (
        (token_mask == 1) | (positions[None, :] == 0)
    )
    rank_in = owner_rank(cand_owner)
    owner_ids = jnp.arange(shard_count, dtype=jnp.int32)
    own_table = slot_table(cand_owner, cand_slot, rank_in, owner_ids, per_owner)
    outgoing_req = jnp.transpose(own_table, (1, 0, 2))
    incoming_req = lax.all_to_all(outgoing_req, "shard", split_axis=0, concat_axis=0, tiled=True)
    requests = incoming_req.reshape(shard_count * query_count, per_owner)
    gathered = lax.all_gather(queries, "shard", axis=0, tiled=True)
    pair_scores = score_pairs(gathered, requests, passages, valid_tok, per_owner)
    returned = lax.all_to_all(
        pair_scores.reshape(shard_count, query_count, per_owner),
        "shard",
        split_axis=0,
        concat_axis=0,
        tiled=True,
    )
    owner_hot = (cand_owner[:, :, None] == owner_ids[None, None, :]).astype(jnp.float32)
    rank_hot = (
        rank_in[:, :, None] == jnp.arange(per_owner, dtype=jnp.int32)[None, None, :]
    ).astype(jnp.float32)
    by_owner = jnp.einsum("qcs,sqr->qcr", owner_hot, returned, precision=lax.Precision.HIGHEST)
    return jnp.sum(by_owner * rank_hot, axis=2)


def solution(mesh):
    in_specs = (
        P(("groups", "shard", "rep"), None, None),
        P(("groups", "shard"), None, None),
        P(("groups", "shard")),
        P(("groups", "shard"), None),
        P(("groups", "shard", "rep"), None),
        P(("groups", "shard", "rep"), None),
    )
    out_specs = P(("groups", "shard", "rep"), None)
    return jax.shard_map(local, mesh=mesh, in_specs=in_specs, out_specs=out_specs, check_vma=False)
```

profile of v0, /device:TPU:0, one launch (start us, length us, event | category | flops | bytes accessed | tf_op | source)
XLA Modules:
  0.0 118.4 jit_solution(4309564102643039008)
XLA Ops:
  1.5 2.6 %convert_reduce_fusion = s32[8,100]{0,1:T(8,128)S(1)} fusion(s32[8,100]{1,0:T(8,128)} %param.12, s32[8,100]{0,1:T(8,128)S(1)} %copy.31, pred[100,100]{1,0:T(8,128)(4,1)S(1)} %iota_compare_fusion.4), kind=kLoop, calls=%fused_computation.21 | loop fusion | flops 319200 | bytes 19600 | tf_op jit(solution)/shard_map/reduce_sum | solution.py:11
  4.9 1.8 %select_reduce_fusion.1 = s32[8,8,13]{1,2,0:T(8,128)S(1)} fusion(s32[8,100]{1,0:T(8,128)S(1)} %broadcast_add_fusion, pred[8,100,13]{1,2,0:T(8,128)(4,1)S(1)} %iota_compare_fusion.3, pred[8,100,8]{1,2,0:T(8,128)(4,1)S(1)} %iota_compare_fusion.5), kind=kLoop, calls=%fused_computation.20 | loop fusion | flops 248768 | bytes 23328 | tf_op jit(solution)/shard_map/reduce_sum | solution.py:18
  7.4 7.3 %all-to-all-start = ((s32[8,8,13]{2,1,0:T(8,128)}), s32[8,8,13]{2,1,0:T(8,128)S(1)}, u32[]{:S(2)}, u32[]{:S(2)}) async-start(s32[8,8,13]{2,1,0:T(8,128)} %copy.33), calls=%async_computation | async-start | bytes 65536 | tf_op jit(solution)/shard_map/all_to_all | solution.py:65
  14.7 34.1 %all_gather.3 = bf16[64,32,128]{2,1,0:T(8,128)(2,1)} all-gather(bf16[8,32,128]{2,1,0:T(8,128)(2,1)} %param.8), channel_id=1, replica_groups=mesh['groups'=2,'shard'=8,'rep'=2] {'shard'}, dimensions={0}, use_global_device_ids=true | all-gather | bytes 589824 | tf_op jit(solution)/shard_map/all_gather | solution.py:67
  48.8 0.9 fusion.18
  49.7 3.9 %copy.34 = bf16[64,192,128]{2,0,1:T(8,128)(2,1)S(1)} copy(bf16[64,192,128]{2,1,0:T(8,128)(2,1)} %param.9) | data formatting | bytes 6291456
  53.7 51.8 %while.11 = (s32[]{:T(128)}, f32[8,8,13]{2,1,0:T(8,128)S(1)}, s32[8,8,13]{2,1,0:T(8,128)S(1)}, bf16[64,192]{1,0:T(8,128)(2,1)S(1)}, bf16[64,192,128]{2,0,1:T(8,1...) while((s32[]{:T(128)}, f32[8,8,13]{2,1,0:T(8,128)S(1)}, ...), condition=%wide.region_5.6_spmd.clone, body=%wide.region_2.5_spmd.clone.sunk | while | flops 497156832 | bytes 13540993 | solution.py:49
  53.7 1.8 %convolution_convert_fusion.2 = bf16[8,13,192,128]{3,1,2,0:T(8,128)(2,1)S(1)} fusion(bf16[64,192,128]{2,0,1:T(8,128)(2,1)S(1)} %get-tuple-element.144, s32[8,13]{1,0:T(8,128)S(1)} %dynamic-slice_bitcast_fusion.2), kind=kOutput, calls=%fused_computation.3.clone.1 | convolution fusion | flops 329718272 | bytes 8257952 | tf_op jit(solution)/shard_map/while/body/eval_jaxpr/bpn,nld->bpld/dot_general | solution.py:36
  55.7 4.3 %select_reduce_fusion.3 = f32[8,13,32]{2,1,0:T(8,128)S(1)} fusion(pred[8,13,192]{2,1,0:T(8,128)(4,1)S(1)} %convolution_compare_fusion.2, bf16[8,13,192,128]{3,1,2,0:T(8,128)(2,1)S(1)} %convolution_convert_fusion.2, bf16[8,8,32,128]{3,2,1,0:T(8,128)(2,1)} %get-tuple-element.145, s32[]{:T(128)} %get-tuple-element.132), kind=kOutput, calls=%fused_computation.4.clone.1 | convolution fusion | flops 164852480 | bytes 5211136 | tf_op jit(solution)/shard_map/while/body/eval_jaxpr/btd,bpld->bptl/dot_general | solution.py:43
  60.2 1.8 %convolution_convert_fusion.2 = bf16[8,13,192,128]{3,1,2,0:T(8,128)(2,1)S(1)} fusion(bf16[64,192,128]{2,0,1:T(8,128)(2,1)S(1)} %get-tuple-element.144, s32[8,13]{1,0:T(8,128)S(1)} %dynamic-slice_bitcast_fusion.2), kind=kOutput, calls=%fused_computation.3.clone.1 | convolution fusion | flops 329718272 | bytes 8257952 | tf_op jit(solution)/shard_map/while/body/eval_jaxpr/bpn,nld->bpld/dot_general | solution.py:36
  62.2 4.3 %select_reduce_fusion.3 = f32[8,13,32]{2,1,0:T(8,128)S(1)} fusion(pred[8,13,192]{2,1,0:T(8,128)(4,1)S(1)} %convolution_compare_fusion.2, bf16[8,13,192,128]{3,1,2,0:T(8,128)(2,1)S(1)} %convolution_convert_fusion.2, bf16[8,8,32,128]{3,2,1,0:T(8,128)(2,1)} %get-tuple-element.145, s32[]{:T(128)} %get-tuple-element.132), kind=kOutput, calls=%fused_computation.4.clone.1 | convolution fusion | flops 164852480 | bytes 5211136 | tf_op jit(solution)/shard_map/while/body/eval_jaxpr/btd,bpld->bptl/dot_general | solution.py:43
  66.6 1.8 %convolution_convert_fusion.2 = bf16[8,13,192,128]{3,1,2,0:T(8,128)(2,1)S(1)} fusion(bf16[64,192,128]{2,0,1:T(8,128)(2,1)S(1)} %get-tuple-element.144, s32[8,13]{1,0:T(8,128)S(1)} %dynamic-slice_bitcast_fusion.2), kind=kOutput, calls=%fused_computation.3.clone.1 | convolution fusion | flops 329718272 | bytes 8257952 | tf_op jit(solution)/shard_map/while/body/eval_jaxpr/bpn,nld->bpld/dot_general | solution.py:36
  68.7 4.3 %select_reduce_fusion.3 = f32[8,13,32]{2,1,0:T(8,128)S(1)} fusion(pred[8,13,192]{2,1,0:T(8,128)(4,1)S(1)} %convolution_compare_fusion.2, bf16[8,13,192,128]{3,1,2,0:T(8,128)(2,1)S(1)} %convolution_convert_fusion.2, bf16[8,8,32,128]{3,2,1,0:T(8,128)(2,1)} %get-tuple-element.145, s32[]{:T(128)} %get-tuple-element.132), kind=kOutput, calls=%fused_computation.4.clone.1 | convolution fusion | flops 164852480 | bytes 5211136 | tf_op jit(solution)/shard_map/while/body/eval_jaxpr/btd,bpld->bptl/dot_general | solution.py:43
  73.1 1.8 %convolution_convert_fusion.2 = bf16[8,13,192,128]{3,1,2,0:T(8,128)(2,1)S(1)} fusion(bf16[64,192,128]{2,0,1:T(8,128)(2,1)S(1)} %get-tuple-element.144, s32[8,13]{1,0:T(8,128)S(1)} %dynamic-slice_bitcast_fusion.2), kind=kOutput, calls=%fused_computation.3.clone.1 | convolution fusion | flops 329718272 | bytes 8257952 | tf_op jit(solution)/shard_map/while/body/eval_jaxpr/bpn,nld->bpld/dot_general | solution.py:36
  75.2 4.3 %select_reduce_fusion.3 = f32[8,13,32]{2,1,0:T(8,128)S(1)} fusion(pred[8,13,192]{2,1,0:T(8,128)(4,1)S(1)} %convolution_compare_fusion.2, bf16[8,13,192,128]{3,1,2,0:T(8,128)(2,1)S(1)} %convolution_convert_fusion.2, bf16[8,8,32,128]{3,2,1,0:T(8,128)(2,1)} %get-tuple-element.145, s32[]{:T(128)} %get-tuple-element.132), kind=kOutput, calls=%fused_computation.4.clone.1 | convolution fusion | flops 164852480 | bytes 5211136 | tf_op jit(solution)/shard_map/while/body/eval_jaxpr/btd,bpld->bptl/dot_general | solution.py:43
  79.6 1.8 %convolution_convert_fusion.2 = bf16[8,13,192,128]{3,1,2,0:T(8,128)(2,1)S(1)} fusion(bf16[64,192,128]{2,0,1:T(8,128)(2,1)S(1)} %get-tuple-element.144, s32[8,13]{1,0:T(8,128)S(1)} %dynamic-slice_bitcast_fusion.2), kind=kOutput, calls=%fused_computation.3.clone.1 | convolution fusion | flops 329718272 | bytes 8257952 | tf_op jit(solution)/shard_map/while/body/eval_jaxpr/bpn,nld->bpld/dot_general | solution.py:36
  81.6 4.3 %select_reduce_fusion.3 = f32[8,13,32]{2,1,0:T(8,128)S(1)} fusion(pred[8,13,192]{2,1,0:T(8,128)(4,1)S(1)} %convolution_compare_fusion.2, bf16[8,13,192,128]{3,1,2,0:T(8,128)(2,1)S(1)} %convolution_convert_fusion.2, bf16[8,8,32,128]{3,2,1,0:T(8,128)(2,1)} %get-tuple-element.145, s32[]{:T(128)} %get-tuple-element.132), kind=kOutput, calls=%fused_computation.4.clone.1 | convolution fusion | flops 164852480 | bytes 5211136 | tf_op jit(solution)/shard_map/while/body/eval_jaxpr/btd,bpld->bptl/dot_general | solution.py:43
  86.1 1.8 %convolution_convert_fusion.2 = bf16[8,13,192,128]{3,1,2,0:T(8,128)(2,1)S(1)} fusion(bf16[64,192,128]{2,0,1:T(8,128)(2,1)S(1)} %get-tuple-element.144, s32[8,13]{1,0:T(8,128)S(1)} %dynamic-slice_bitcast_fusion.2), kind=kOutput, calls=%fused_computation.3.clone.1 | convolution fusion | flops 329718272 | bytes 8257952 | tf_op jit(solution)/shard_map/while/body/eval_jaxpr/bpn,nld->bpld/dot_general | solution.py:36
  88.1 4.3 %select_reduce_fusion.3 = f32[8,13,32]{2,1,0:T(8,128)S(1)} fusion(pred[8,13,192]{2,1,0:T(8,128)(4,1)S(1)} %convolution_compare_fusion.2, bf16[8,13,192,128]{3,1,2,0:T(8,128)(2,1)S(1)} %convolution_convert_fusion.2, bf16[8,8,32,128]{3,2,1,0:T(8,128)(2,1)} %get-tuple-element.145, s32[]{:T(128)} %get-tuple-element.132), kind=kOutput, calls=%fused_computation.4.clone.1 | convolution fusion | flops 164852480 | bytes 5211136 | tf_op jit(solution)/shard_map/while/body/eval_jaxpr/btd,bpld->bptl/dot_general | solution.py:43
  92.5 1.8 %convolution_convert_fusion.2 = bf16[8,13,192,128]{3,1,2,0:T(8,128)(2,1)S(1)} fusion(bf16[64,192,128]{2,0,1:T(8,128)(2,1)S(1)} %get-tuple-element.144, s32[8,13]{1,0:T(8,128)S(1)} %dynamic-slice_bitcast_fusion.2), kind=kOutput, calls=%fused_computation.3.clone.1 | convolution fusion | flops 329718272 | bytes 8257952 | tf_op jit(solution)/shard_map/while/body/eval_jaxpr/bpn,nld->bpld/dot_general | solution.py:36
  94.6 4.3 %select_reduce_fusion.3 = f32[8,13,32]{2,1,0:T(8,128)S(1)} fusion(pred[8,13,192]{2,1,0:T(8,128)(4,1)S(1)} %convolution_compare_fusion.2, bf16[8,13,192,128]{3,1,2,0:T(8,128)(2,1)S(1)} %convolution_convert_fusion.2, bf16[8,8,32,128]{3,2,1,0:T(8,128)(2,1)} %get-tuple-element.145, s32[]{:T(128)} %get-tuple-element.132), kind=kOutput, calls=%fused_computation.4.clone.1 | convolution fusion | flops 164852480 | bytes 5211136 | tf_op jit(solution)/shard_map/while/body/eval_jaxpr/btd,bpld->bptl/dot_general | solution.py:43
  99.0 1.8 %convolution_convert_fusion.2 = bf16[8,13,192,128]{3,1,2,0:T(8,128)(2,1)S(1)} fusion(bf16[64,192,128]{2,0,1:T(8,128)(2,1)S(1)} %get-tuple-element.144, s32[8,13]{1,0:T(8,128)S(1)} %dynamic-slice_bitcast_fusion.2), kind=kOutput, calls=%fused_computation.3.clone.1 | convolution fusion | flops 329718272 | bytes 8257952 | tf_op jit(solution)/shard_map/while/body/eval_jaxpr/bpn,nld->bpld/dot_general | solution.py:36
  101.1 4.3 %select_reduce_fusion.3 = f32[8,13,32]{2,1,0:T(8,128)S(1)} fusion(pred[8,13,192]{2,1,0:T(8,128)(4,1)S(1)} %convolution_compare_fusion.2, bf16[8,13,192,128]{3,1,2,0:T(8,128)(2,1)S(1)} %convolution_convert_fusion.2, bf16[8,8,32,128]{3,2,1,0:T(8,128)(2,1)} %get-tuple-element.145, s32[]{:T(128)} %get-tuple-element.132), kind=kOutput, calls=%fused_computation.4.clone.1 | convolution fusion | flops 164852480 | bytes 5211136 | tf_op jit(solution)/shard_map/while/body/eval_jaxpr/btd,bpld->bptl/dot_general | solution.py:43
  105.5 12.1 %all_to_all.10 = f32[8,8,13]{2,1,0:T(8,128)S(1)} all-to-all(f32[8,8,13]{2,1,0:T(8,128)S(1)} %get-tuple-element.42), channel_id=1, replica_groups=mesh['groups'=2,'shard'=8,'rep'=2] {'shard'}, dimensions={0} | all-to-all | bytes 6656 | tf_op jit(solution)/shard_map/all_to_all | solution.py:69
  (46 shorter events, 6.5 us)
Async XLA Ops:
  7.4 46.2 %all-to-all-start = ((s32[8,8,13]{2,1,0:T(8,128)}), s32[8,8,13]{2,1,0:T(8,128)S(1)}, u32[]{:S(2)}, u32[]{:S(2)}) async-start(s32[8,8,13]{2,1,0:T(8,128)} %copy.33), calls=%async_computation | async-start | bytes 65536 | tf_op jit(solution)/shard_map/all_to_all | solution.py:65
  53.6 63.9 %copy-start = (s32[8,100]{1,0:T(8,128)S(1)}, s32[8,100]{1,0:T(8,128)}, u32[]{:S(2)}) copy-start(s32[8,100]{1,0:T(8,128)} %param.12) | copy-start | bytes 9604
where the time goes:
time: 119 us; the launch traced here: 118 us
  matrix products  51.3 us (43%)
  blocking collectives  46.2 us (39%)
  other arithmetic  7.66 us (6%)
  starting transfers between devices  7.25 us (6%)
  local copies, waits for them, and re-layouts  5.56 us (5%)
    dot_general x8, matrix products, score_block(): jnp.einsum('btd,bpld->bptl', query_tok, passage_tok, preferred_element_ty...  34.1 us
    all_gather x1, blocking collectives, local(): gathered = lax.all_gather(queries, 'shard', axis=0, tiled=True)  34.1 us
    dot_general x8, matrix products, score_block(): jnp.einsum('bpn,nld->bpld', one_hot.astype(passages.dtype), passages, pre...  14.7 us
    all_to_all x1, blocking collectives, local(): lax.all_to_all(pair_scores.reshape(shard_count, query_count, per_owner),...  12.1 us
    all_to_all x1, starting transfers between devices, local(): lax.all_to_all(outgoing_req, 'shard', split_axis=0, concat_axis=0, tiled=...  7.25 us
    unnamed x4, local copies, waits for them, and re-layouts  4.72 us
    reduce_sum x1, other arithmetic, owner_rank(): return jnp.sum(same_owner & earlier[None], axis=2)  2.57 us
  transfers between devices with their start and end apart: 1, of which 0 were waited for; matrix products, arithmetic and copies ran while one was open for 4% of the time, Pallas kernels for 0%

commit v1 on v0

v1 whole, which is shorter than its diff:
```python
import functools

import jax
import jax.numpy as jnp
from jax import lax
from jax.experimental import pallas as pl
from jax.experimental.pallas import tpu as pltpu
from jax.sharding import PartitionSpec as P

NT = (((1,), (1,)), ((), ()))
CHUNK = 4
MASKED = -1e30


def token_bias(lengths, mask):
    slots, tokens = mask.shape
    positions = lax.broadcasted_iota(jnp.int32, (tokens, slots), 0)
    taken = mask.astype(jnp.float32).T > 0.5
    valid = (positions < lengths.reshape(1, slots)) & (taken | (positions == 0))
    bias = jnp.where(valid, 0.0, MASKED)
    return jnp.concatenate([bias, jnp.zeros((tokens, 128 - slots), jnp.float32)], axis=1).astype(jnp.bfloat16)


def best_matches(passages, bias, query_rows, best):
    slots, tokens, _ = passages.shape
    columns = query_rows.shape[0]
    weights = jnp.concatenate([query_rows, jnp.ones((columns, 128), jnp.bfloat16)], axis=1)
    lane = lax.broadcasted_iota(jnp.int32, (tokens, 128), 1)
    for first in range(0, slots, CHUNK):
        rows = [
            jnp.concatenate([passages[p], jnp.where(lane == p, bias, 0).astype(jnp.bfloat16)], axis=1)
            for p in range(first, first + CHUNK)
        ]
        similar = lax.dot_general(jnp.concatenate(rows, axis=0), weights, NT, preferred_element_type=jnp.float32)
        best[first : first + CHUNK] = jnp.max(similar.reshape(CHUNK, tokens // 8, 8, columns), axis=1)


def token_means(best, count, token_count):
    columns = best.shape[1]
    row = lax.broadcasted_iota(jnp.int32, (count, columns), 0)
    column = lax.broadcasted_iota(jnp.int32, (count, columns), 1)
    pick = (row == lax.div(column, token_count)).astype(jnp.bfloat16)
    total = jnp.zeros((count, best.shape[0]), jnp.float32)
    rest = best
    for _ in range(3):
        part = rest.astype(jnp.bfloat16)
        total = total + lax.dot_general(pick, part, NT, preferred_element_type=jnp.float32)
        rest = rest - part.astype(jnp.float32)
    return total * (1.0 / token_count)


def score_kernel(token_count, first, count, passages, lengths, mask, queries, out, best):
    bias = token_bias(lengths[...], mask[...])
    for start in range(first, first + count, 8):
        rows = queries[start * token_count : (start + 8) * token_count, :]
        best_matches(passages, bias, rows, best)
        out[start - first : start - first + 8, :] = token_means(jnp.max(best[...], axis=1), 8, token_count)


def score(passages, lengths, mask, queries, token_count, first, count):
    slots = passages.shape[0]
    return pl.pallas_call(
        functools.partial(score_kernel, token_count, first, count),
        out_shape=jax.ShapeDtypeStruct((count, slots), jnp.float32),
        in_specs=[pl.BlockSpec(memory_space=pltpu.VMEM)] * 4,
        out_specs=pl.BlockSpec(memory_space=pltpu.VMEM),
        scratch_shapes=[pltpu.VMEM((slots, 8, 8 * token_count), jnp.float32)],
        compiler_params=pltpu.CompilerParams(vmem_limit_bytes=16 * 2**20),
        cost_estimate=pl.CostEstimate(
            flops=2 * count * token_count * slots * passages.shape[1] * 256,
            bytes_accessed=passages.size * 2,
            transcendentals=0,
        ),
    )(passages, lengths, mask, queries)


def select_kernel(returned, owner, slot, out):
    owners, _, slots = returned.shape
    count = owner.shape[1]
    pad = ((0, 0), (0, 128 - count))
    own = jnp.concatenate([owner[...], jnp.zeros((owner.shape[0], 128 - count), jnp.int32)], axis=1)
    at = jnp.concatenate([slot[...], jnp.zeros((owner.shape[0], 128 - count), jnp.int32)], axis=1)
    del pad
    total = jnp.zeros(own.shape, jnp.float32)
    for s in range(owners):
        row = jnp.concatenate([returned[s], returned[s]], axis=1)
        total = jnp.where(own == s, jnp.take_along_axis(row, at, axis=1, mode="promise_in_bounds"), total)
    out[...] = total[:, :count]


def select(returned, owner, slot):
    return pl.pallas_call(
        select_kernel,
        out_shape=jax.ShapeDtypeStruct(owner.shape, jnp.float32),
        in_specs=[pl.BlockSpec(memory_space=pltpu.VMEM)] * 3,
        out_specs=pl.BlockSpec(memory_space=pltpu.VMEM),
    )(returned, owner, slot)


def local(queries, passages, lengths, token_mask, cand_owner, cand_slot):
    shard_count = lax.axis_size("shard")
    query_count, token_count, dim = queries.shape
    rows = queries.reshape(query_count * token_count, dim)
    slots = passages.shape[0]
    if shard_count == 8:
        swap = lambda x, d: lax.ppermute(x, "shard", [(i, i ^ d) for i in range(shard_count)])
        far, mid, near = swap(rows, 4), swap(rows, 6), swap(rows, 2)
        line = jnp.concatenate([rows, near, far, mid], axis=0)
        other = swap(line, 1)
        run = functools.partial(score, passages, lengths, token_mask, token_count=token_count)
        own_scores = run(rows, first=0, count=query_count)
        line_scores = run(line, first=query_count, count=3 * query_count)
        other_scores = run(other, first=0, count=4 * query_count)
        by_step = jnp.concatenate([own_scores, line_scores, other_scores], axis=0).reshape(8, query_count, slots)
        me = lax.axis_index("shard")
        order = jnp.array([0, 2, 4, 6, 1, 3, 5, 7])
        place = jnp.argsort(order)
        by_dest = by_step[place[jnp.arange(8) ^ me]]
    else:
        every = lax.all_gather(rows, "shard", axis=0, tiled=True)

        def step(part):
            return score(passages, lengths, token_mask, part, token_count, 0, query_count)

        by_dest = lax.map(step, every.reshape(shard_count, query_count * token_count, dim))
    returned = lax.all_to_all(by_dest, "shard", split_axis=0, concat_axis=0, tiled=True)
    return select(returned, cand_owner, cand_slot)


def solution(mesh):
    in_specs = (
        P(("groups", "shard", "rep"), None, None),
        P(("groups", "shard"), None, None),
        P(("groups", "shard")),
        P(("groups", "shard"), None),
        P(("groups", "shard", "rep"), None),
        P(("groups", "shard", "rep"), None),
    )
    out_specs = P(("groups", "shard", "rep"), None)
    return jax.shard_map(local, mesh=mesh, in_specs=in_specs, out_specs=out_specs, check_vma=False)
```

time: 119 us -> 45.2 us (0.38)
  matrix products: 51.3 us -> 0 us
  blocking collectives: 46.2 us -> 12.1 us
  Pallas kernels: 0 us -> 17 us
  other arithmetic: 7.66 us -> 0.75 us
  local copies, waits for them, and re-layouts: 5.56 us -> 7.38 us
    dot_general x25 -> x0, matrix products: 51.3 us -> none  [the longest x8 34.1 us: score_block(): jnp.einsum('btd,bpld->bptl', query_tok, passage_tok, preferred_element_ty...]
    all_gather x1 -> x0, blocking collectives: 34.1 us -> none  [local(): gathered = lax.all_gather(queries, 'shard', axis=0, tiled=True)]
    pallas_call x0 -> x4, Pallas kernels: none -> 17 us  [the longest x3 15.5 us: score(): pl.pallas_call(functools.partial(score_kernel, token_count, first, count)...]
    ppermute x0 -> x4, starting transfers between devices: none -> 7.39 us  [local(): lax.ppermute(x, 'shard', [(i, i ^ d) for i in range(shard_count)])]
    all_to_all x1 -> x0, starting transfers between devices: 7.25 us -> none  [local(): lax.all_to_all(outgoing_req, 'shard', split_axis=0, concat_axis=0, tiled=...]
    reduce_sum x10 -> x0, other arithmetic: 5.21 us -> none  [the longest x1 2.57 us: owner_rank(): return jnp.sum(same_owner & earlier[None], axis=2)]
    gather x0 -> x2, local copies, waits for them, and re-layouts: none -> 1.88 us  [local(): by_dest = by_step[place[jnp.arange(8) ^ me]]]
    unnamed x4 -> x10, local copies, waits for them, and re-layouts: 4.72 us -> 4.98 us
  transfers between devices with their start and end apart: 1 -> 4, of which waited for: 0 -> 0; matrix products, arithmetic and copies ran while one was open for 4% -> 3% of each run, Pallas kernels for 0% -> 17%
where the time goes in v1:
time: 45.2 us; the launch traced here: 44.8 us
  Pallas kernels  17 us (38%)
  blocking collectives  12.1 us (27%)
  starting transfers between devices  7.39 us (16%)
  local copies, waits for them, and re-layouts  7.38 us (16%)
  other arithmetic  0.75 us (2%)
    pallas_call x3, Pallas kernels, score(): pl.pallas_call(functools.partial(score_kernel, token_count, first, count)...  15.5 us
    all_to_all x1, blocking collectives, local(): lax.all_to_all(by_dest, 'shard', split_axis=0, concat_axis=0, tiled=True)  12.1 us
    ppermute x4, starting transfers between devices, local(): lax.ppermute(x, 'shard', [(i, i ^ d) for i in range(shard_count)])  7.39 us
    unnamed x10, local copies, waits for them, and re-layouts  4.98 us
    gather x2, local copies, waits for them, and re-layouts, local(): by_dest = by_step[place[jnp.arange(8) ^ me]]  1.88 us
    pallas_call x1, Pallas kernels, select(): pl.pallas_call(select_kernel, out_shape=jax.ShapeDtypeStruct(owner.shape,...  1.52 us
  transfers between devices with their start and end apart: 4, of which 0 were waited for; matrix products, arithmetic and copies ran while one was open for 3% of the time, Pallas kernels for 17%

profile of v1, /device:TPU:0, one launch (start us, length us, event | category | flops | bytes accessed | tf_op | source)
XLA Modules:
  0.0 44.8 jit_solution(12178419154178395715)
XLA Ops:
  0.0 3.0 %collective-permute-start = (bf16[256,128]{1,0:T(8,128)(2,1)}, bf16[256,128]{1,0:T(8,128)(2,1)S(1)}, u32[]{:S(2)}, u32[]{:S(2)}) collective-permute-start(bf16[256,128]{1,0:T(8,128)(2,1)} %bitcast.9), channel_id=1, source_target_pairs={{0,4},{2,6},{4,0},{6,2},{8,12},{10,14},{12,8},{14,10},{1,5},{3,7},... | collective-permute-start | bytes 196616 | tf_op jit(solution)/shard_map/ppermute | solution.py:106
  3.0 2.6 %collective-permute-start.1 = (bf16[256,128]{1,0:T(8,128)(2,1)}, bf16[256,128]{1,0:T(8,128)(2,1)S(1)}, u32[]{:S(2)}, u32[]{:S(2)}) collective-permute-start(bf16[256,128]{1,0:T(8,128)(2,1)} %bitcast.10), channel_id=1, source_target_pairs={{0,8},{2,10},{4,12},{6,14},{8,0},{10,2},{12,4},{14,6},{1,9},{3,11}... | collective-permute-start | bytes 196616 | tf_op jit(solution)/shard_map/ppermute | solution.py:106
  5.6 0.0 collective-permute-start.2
  5.6 1.3 %gather_fusion = s32[8]{0:T(128)S(1)} fusion(s32[8]{0:T(128)} %constant.17, s32[1024]{0:T(1024)S(1)} %pad_clamp_fusion.1), kind=kCustom, calls=%fused_computation | custom fusion | bytes 96 | tf_op jit(solution)/shard_map/gather | solution.py:118
  6.9 0.0 copy-start
  7.0 0.8 %copy-done = bf16[8,32,128]{2,1,0:T(8,128)(2,1)S(1)} copy-done((bf16[8,32,128]{2,1,0:T(8,128)(2,1)S(1)}, bf16[8,32,128]{2,1,0:T(8,128)(2,1)}, u32[]{:S(2)}) %copy-start) | copy-done | bytes 65560
  7.8 1.9 %copy-done.1 = bf16[64,192,128]{2,1,0:T(8,128)(2,1)S(1)} copy-done((bf16[64,192,128]{2,1,0:T(8,128)(2,1)S(1)}, bf16[64,192,128]{2,1,0:T(8,128)(2,1)}, u32[]{:S(2)}) %copy-start.1) | copy-done | bytes 3145752
  9.7 0.8 %copy-done.2 = s32[64,192]{1,0:T(8,128)S(1)} copy-done((s32[64,192]{1,0:T(8,128)S(1)}, s32[64,192]{1,0:T(8,128)}, u32[]{:S(2)}) %copy-start.2) | copy-done | bytes 49176
  10.5 0.7 %copy-done.3 = s32[64]{0:T(128)S(1)} copy-done((s32[64]{0:T(128)S(1)}, s32[64]{0:T(128)}, u32[]{:S(2)}) %copy-start.3) | copy-done | bytes 280
  11.2 2.0 %shard_map.73 = f32[8,64]{1,0:T(8,128)S(1)} custom-call(bf16[64,192,128]{2,1,0:T(8,128)(2,1)S(1)} %copy-done.1, s32[64]{0:T(128)S(1)} %copy-done.3, s32[64,192]{1,0:T(8,128)S(1)} %copy-done.2, bf16[256,128]{1,0:T(8,128)(2,1)S(1)} %bitcast.12), custom_call_target="tpu_custom_call" | custom-call | flops 1610612736 | bytes 3145728 | tf_op jit(solution)/shard_map/pallas_call | solution.py:62
  13.2 0.0 collective-permute-done
  13.2 0.0 collective-permute-done.1
  13.2 0.0 collective-permute-done.2
  13.2 1.8 %collective-permute-start.3 = (bf16[1024,128]{1,0:T(8,128)(2,1)S(1)}, bf16[1024,128]{1,0:T(8,128)(2,1)S(1)}, u32[]{:S(2)}, u32[]{:S(2)}) collective-permute-start(bf16[1024,128]{1,0:T(8,128)(2,1)S(1)} %pad_maximum_fusion.queries), channel_id=1, source_target_pairs={{0,2},{2,0},{4,6},{6,4},{8,10},{10,8},{12,14},{14,12},{1,3},{3,1},... | collective-permute-start | bytes 786440 | tf_op jit(solution)/shard_map/ppermute | solution.py:106
  15.0 5.7 %shard_map.74 = f32[24,64]{1,0:T(8,128)S(1)} custom-call(bf16[64,192,128]{2,1,0:T(8,128)(2,1)S(1)} %copy-done.1, s32[64]{0:T(128)S(1)} %copy-done.3, s32[64,192]{1,0:T(8,128)S(1)} %copy-done.2, bf16[1024,128]{1,0:T(8,128)(2,1)S(1)} %pad_maximum_fusion.queries), custom_call_target="tpu_custom_call" | custom-call | flops 4831838208 | bytes 3145728 | tf_op jit(solution)/shard_map/pallas_call | solution.py:62
  20.7 0.0 collective-permute-done.3.queries
  20.8 7.8 %shard_map.75 = f32[32,64]{1,0:T(8,128)S(1)} custom-call(bf16[64,192,128]{2,1,0:T(8,128)(2,1)S(1)} %copy-done.1, s32[64]{0:T(128)S(1)} %copy-done.3, s32[64,192]{1,0:T(8,128)S(1)} %copy-done.2, bf16[1024,128]{1,0:T(8,128)(2,1)S(1)} %collective-permute-done.3.queries), custom_call_target="tpu_custom_call" | custom-call | flops 6442450944 | bytes 3145728 | tf_op jit(solution)/shard_map/pallas_call | solution.py:62
  28.6 0.6 %gather_fusion.1 = f32[8,8,64]{2,1,0:T(8,128)S(1)} fusion(f32[8,8,64]{2,1,0:T(8,128)S(1)} %maximum_bitcast_fusion, s32[1024]{0:T(1024)S(1)} %pad_clamp_fusion), kind=kCustom, calls=%fused_computation.1 | custom fusion | bytes 32800 | tf_op jit(solution)/shard_map/gather | solution.py:118
  29.2 0.1 reshape.53
  29.3 12.1 %all_to_all.5 = f32[8,1,512]{2,1,0:T(1,128)S(1)} all-to-all(f32[8,1,512]{2,1,0:T(1,128)S(1)} %reshape.53), channel_id=1, replica_groups=mesh['groups'=2,'shard'=8,'rep'=2] {'shard'}, dimensions={0} | all-to-all | bytes 32768 | tf_op jit(solution)/shard_map/all_to_all | solution.py:126
  41.4 0.5 %broadcast.55 = f32[]{:T(128)} broadcast(f32[]{:T(128)} %constant.36), dimensions={} | broadcast | bytes 8 | tf_op jit(solution)/shard_map/all_to_all | solution.py:126
  41.9 0.7 %reduce = f32[8,512]{1,0:T(8,128)S(1)} reduce(f32[8,1,512]{2,1,0:T(1,128)S(1)} %all_to_all.5, f32[]{:T(128)} %broadcast.55), dimensions={1}, to_apply=%all_to_all.3.reduce_sub_computation | reduce | bytes 32772 | tf_op jit(solution)/shard_map/all_to_all | solution.py:126
  42.6 0.7 %reshape.54.returned = f32[8,8,64]{2,1,0:T(8,128)} reshape(f32[8,512]{1,0:T(8,128)S(1)} %reduce) | data formatting | bytes 32768
  43.3 1.5 %shard_map.76 = f32[8,100]{1,0:T(8,128)} custom-call(f32[8,8,64]{2,1,0:T(8,128)} %reshape.54.returned, s32[8,100]{1,0:T(8,128)} %owner.1, s32[8,100]{1,0:T(8,128)} %slot.1), custom_call_target="tpu_custom_call" | custom-call | tf_op jit(solution)/shard_map/pallas_call | solution.py:92
  (9 shorter events, 0.1 us)
Async XLA Ops:
  0.0 13.2 %collective-permute-start = (bf16[256,128]{1,0:T(8,128)(2,1)}, bf16[256,128]{1,0:T(8,128)(2,1)S(1)}, u32[]{:S(2)}, u32[]{:S(2)}) collective-permute-start(bf16[256,128]{1,0:T(8,128)(2,1)} %bitcast.9), channel_id=1, source_target_pairs={{0,4},{2,6},{4,0},{6,2},{8,12},{10,14},{12,8},{14,10},{1,5},{3,7},... | collective-permute-start | bytes 196616 | tf_op jit(solution)/shard_map/ppermute | solution.py:106
  3.0 10.2 %collective-permute-start.1 = (bf16[256,128]{1,0:T(8,128)(2,1)}, bf16[256,128]{1,0:T(8,128)(2,1)S(1)}, u32[]{:S(2)}, u32[]{:S(2)}) collective-permute-start(bf16[256,128]{1,0:T(8,128)(2,1)} %bitcast.10), channel_id=1, source_target_pairs={{0,8},{2,10},{4,12},{6,14},{8,0},{10,2},{12,4},{14,6},{1,9},{3,11}... | collective-permute-start | bytes 196616 | tf_op jit(solution)/shard_map/ppermute | solution.py:106
  5.6 7.6 %collective-permute-start.2 = (bf16[256,128]{1,0:T(8,128)(2,1)}, bf16[256,128]{1,0:T(8,128)(2,1)S(1)}, u32[]{:S(2)}, u32[]{:S(2)}) collective-permute-start(bf16[256,128]{1,0:T(8,128)(2,1)} %bitcast.11), channel_id=1, source_target_pairs={{0,12},{2,14},{4,8},{6,10},{8,4},{10,6},{12,0},{14,2},{1,13},{3,15... | collective-permute-start | bytes 196616 | tf_op jit(solution)/shard_map/ppermute | solution.py:106
  6.9 0.8 %copy-start = (bf16[8,32,128]{2,1,0:T(8,128)(2,1)S(1)}, bf16[8,32,128]{2,1,0:T(8,128)(2,1)}, u32[]{:S(2)}) copy-start(bf16[8,32,128]{2,1,0:T(8,128)(2,1)} %param.7) | copy-start | bytes 196612
  7.8 1.9 %copy-start.1 = (bf16[64,192,128]{2,1,0:T(8,128)(2,1)S(1)}, bf16[64,192,128]{2,1,0:T(8,128)(2,1)}, u32[]{:S(2)}) copy-start(bf16[64,192,128]{2,1,0:T(8,128)(2,1)} %passages.5) | copy-start | bytes 9437188
  9.7 0.8 %copy-start.2 = (s32[64,192]{1,0:T(8,128)S(1)}, s32[64,192]{1,0:T(8,128)}, u32[]{:S(2)}) copy-start(s32[64,192]{1,0:T(8,128)} %mask.5) | copy-start | bytes 147460
  10.5 0.7 %copy-start.3 = (s32[64]{0:T(128)S(1)}, s32[64]{0:T(128)}, u32[]{:S(2)}) copy-start(s32[64]{0:T(128)} %lengths.5) | copy-start | bytes 772
  13.2 7.6 %collective-permute-start.3 = (bf16[1024,128]{1,0:T(8,128)(2,1)S(1)}, bf16[1024,128]{1,0:T(8,128)(2,1)S(1)}, u32[]{:S(2)}, u32[]{:S(2)}) collective-permute-start(bf16[1024,128]{1,0:T(8,128)(2,1)S(1)} %pad_maximum_fusion.queries), channel_id=1, source_target_pairs={{0,2},{2,0},{4,6},{6,4},{8,10},{10,8},{12,14},{14,12},{1,3},{3,1},... | collective-permute-start | bytes 786440 | tf_op jit(solution)/shard_map/ppermute | solution.py:106

commit v2 on v1

v2 whole, which is shorter than its diff:
```python
import functools

import jax
import jax.numpy as jnp
from jax import lax
from jax.experimental import pallas as pl
from jax.experimental.pallas import tpu as pltpu
from jax.sharding import PartitionSpec as P

NT = (((1,), (1,)), ((), ()))
LANES = 128
GROUP = 8
REQUEST_ROWS = 16
EXTRA = 16
VMEM = pl.BlockSpec(memory_space=pltpu.VMEM)
HBM = pl.BlockSpec(memory_space=pltpu.HBM)


def in_hbm(*arrays):
    return [pltpu.with_memory_space_constraint(a, pltpu.HBM) for a in arrays]


def params(mib):
    return pltpu.CompilerParams(vmem_limit_bytes=mib * 2**20)


def wide(values, fill):
    return jnp.concatenate([values, jnp.full((values.shape[0], LANES - values.shape[1]), fill, values.dtype)], axis=1)


def pack_kernel(rows, owner, slot, out, owner_here, slot_here, sems):
    count = rows.shape[0]
    copies = [
        pltpu.make_async_copy(rows, out.at[pl.ds(0, count)], sems.at[0]),
        pltpu.make_async_copy(owner, owner_here, sems.at[1]),
        pltpu.make_async_copy(slot, slot_here, sems.at[2]),
    ]
    for copy in copies:
        copy.start()
    copies[1].wait()
    copies[2].wait()
    named = jnp.concatenate([wide(owner_here[...], -1), wide(slot_here[...], 0)], axis=0)
    out[count:, :] = named.astype(jnp.float32).astype(jnp.bfloat16)
    copies[0].wait()


def pack(rows, owner, slot):
    return pl.pallas_call(
        pack_kernel,
        out_shape=pltpu.VMEM((rows.shape[0] + REQUEST_ROWS, LANES), jnp.bfloat16),
        in_specs=[HBM] * 3,
        out_specs=VMEM,
        scratch_shapes=[
            pltpu.VMEM(owner.shape, jnp.int32),
            pltpu.VMEM(slot.shape, jnp.int32),
            pltpu.SemaphoreType.DMA((3,)),
        ],
        compiler_params=params(4),
    )(*in_hbm(rows, owner, slot))


def fill_kernel(passages, lengths, mask, out, mask_here, lengths_here, sems):
    slots, tokens, _ = passages.shape
    parts = 8
    each = slots // parts
    head = [
        pltpu.make_async_copy(mask, mask_here, sems.at[parts]),
        pltpu.make_async_copy(lengths, lengths_here, sems.at[parts + 1]),
    ]
    copies = [
        pltpu.make_async_copy(passages.at[pl.ds(i * each, each)], out.at[pl.ds(i * each, each)], sems.at[i])
        for i in range(parts)
    ]
    for copy in head + copies:
        copy.start()
    for copy in head:
        copy.wait()
    positions = lax.broadcasted_iota(jnp.int32, (tokens, slots), 0)
    taken = mask_here[...].astype(jnp.float32).T > 0.5
    valid = (positions < lengths_here[...].reshape(1, slots)) & (taken | (positions == 0))
    valid = wide(jnp.where(valid, 1.0, 0.0), 0.0).astype(jnp.bfloat16)
    lane = lax.broadcasted_iota(jnp.int32, (tokens, LANES), 1)
    ones = jnp.ones((LANES, LANES), jnp.bfloat16)
    for i in range(parts):
        copies[i].wait()
        for p in range(i * each, (i + 1) * each):
            one = jnp.where(lane == p, valid, 0).astype(jnp.bfloat16)
            keep = jnp.dot(one, ones, preferred_element_type=jnp.float32) > 0.5
            tok = out[p].astype(jnp.float32)
            out[p] = jnp.where(keep, tok, tok[0:1]).astype(jnp.bfloat16)


def fill(passages, lengths, mask):
    return pl.pallas_call(
        fill_kernel,
        out_shape=pltpu.VMEM(passages.shape, jnp.bfloat16),
        in_specs=[HBM] * 3,
        out_specs=VMEM,
        scratch_shapes=[
            pltpu.VMEM(mask.shape, jnp.int32),
            pltpu.VMEM(lengths.shape, jnp.int32),
            pltpu.SemaphoreType.DMA((10,)),
        ],
        compiler_params=params(16),
        cost_estimate=pl.CostEstimate(flops=0, bytes_accessed=passages.size * 4, transcendentals=0),
    )(*in_hbm(passages, lengths, mask))


def request_tables(blocks, me, block_rows, block_count, tokens, cand_count, slots):
    per_block = REQUEST_ROWS // 2
    queries = block_count * per_block
    target = []
    for b in range(block_count):
        first = b * block_rows + block_rows - REQUEST_ROWS
        request = blocks[first : first + REQUEST_ROWS, :].astype(jnp.float32)
        target.append(jnp.where(request[:per_block] == me, request[per_block:], -1.0))
    target = jnp.concatenate(target, axis=0)
    lane = lax.broadcasted_iota(jnp.int32, (queries, LANES), 1).astype(jnp.float32)
    named = jnp.zeros((queries, LANES), jnp.float32)
    for c in range(cand_count):
        named = jnp.where(target[:, c : c + 1] == lane, 1.0, named)
    row = lax.broadcasted_iota(jnp.int32, (queries, queries), 0)
    column = lax.broadcasted_iota(jnp.int32, (queries, queries), 1)
    earlier = (column < row).astype(jnp.bfloat16)
    rank = jnp.dot(earlier, named.astype(jnp.bfloat16), preferred_element_type=jnp.float32)
    rank = jnp.where(named > 0.5, rank, -1.0)
    number = lax.broadcasted_iota(jnp.int32, (queries, LANES), 0)
    place = lax.div(number, per_block) * block_rows + lax.rem(number, per_block) * tokens
    place = place.astype(jnp.float32)
    lists = [jnp.sum(jnp.where(rank == r, place, 0.0), axis=0, keepdims=True) for r in range(queries)]
    count = jnp.sum(named, axis=0, keepdims=True)
    return rank, jnp.concatenate(lists, axis=0).astype(jnp.int32), count


def overflow_list(count, slots, most):
    capacity = slots * (most - 1)
    later = jnp.maximum(jnp.floor((count + (GROUP - 1)) * (1.0 / GROUP)) - 1.0, 0.0)
    later = jnp.broadcast_to(later, (8, LANES))
    row = lax.broadcasted_iota(jnp.int32, (LANES, LANES), 0)
    column = lax.broadcasted_iota(jnp.int32, (LANES, LANES), 1)
    before = jnp.dot(later.astype(jnp.bfloat16), (row < column).astype(jnp.bfloat16), preferred_element_type=jnp.float32)
    entry = lax.broadcasted_iota(jnp.int32, (capacity, LANES), 0).astype(jnp.float32)
    mine = ((before[0:1] <= entry) & (entry < before[0:1] + later[0:1])).astype(jnp.bfloat16)
    passage = lax.broadcasted_iota(jnp.int32, (8, LANES), 1).astype(jnp.float32)
    kind = lax.broadcasted_iota(jnp.int32, (8, LANES), 0)
    facts = jnp.where(kind == 0, passage, jnp.where(kind == 1, before, later)).astype(jnp.bfloat16)
    found = lax.dot_general(facts, mine, NT, preferred_element_type=jnp.float32)
    total = jnp.sum(later[0:1], axis=1, keepdims=True)
    at = lax.broadcasted_iota(jnp.int32, (1, capacity), 1).astype(jnp.float32)
    group = jnp.clip(at - found[1:2] + 1.0, 1.0, float(most - 1))
    total = jnp.broadcast_to(total, (1, capacity))
    return jnp.concatenate([found[0:1], group, total], axis=0).astype(jnp.int32)


def token_means(best, tokens):
    columns = best.shape[1]
    row = lax.broadcasted_iota(jnp.int32, (GROUP, columns), 0)
    column = lax.broadcasted_iota(jnp.int32, (GROUP, columns), 1)
    pick = (row == lax.div(column, tokens)).astype(jnp.bfloat16)
    total = jnp.zeros((GROUP, best.shape[0]), jnp.float32)
    rest = best
    for _ in range(3):
        part = rest.astype(jnp.bfloat16)
        total = total + lax.dot_general(pick, part, NT, preferred_element_type=jnp.float32)
        rest = rest - part.astype(jnp.float32)
    return total * (1.0 / tokens)


def score_blocks(
    block_rows, block_count, tokens, cand_count, me, passages, blocks,
    best, table, lists_here, lists, extras_here, extras, sems,
):
    slots, length, dim = passages.shape
    queries = block_count * (REQUEST_ROWS // 2)
    most = queries // GROUP
    rank, listed, count = request_tables(blocks, me, block_rows, block_count, tokens, cand_count, slots)
    capacity = slots * (most - 1)
    lists_here[...] = listed
    copies = [pltpu.make_async_copy(lists_here.at[pl.ds(0, GROUP)], lists.at[pl.ds(0, GROUP)], sems.at[0])]
    copies[0].start()
    if most > 1:
        later = pl.ds(GROUP, queries - GROUP)
        copies.append(pltpu.make_async_copy(lists_here.at[later], lists.at[later], sems.at[1]))
        extras_here[0:3, 0:capacity] = overflow_list(count, slots, most)
        copies.append(pltpu.make_async_copy(extras_here, extras, sems.at[2]))
        copies[1].start()
        copies[2].start()
    copies[0].wait()

    def group_best(p, first):
        rows = [blocks[pl.ds(pl.multiple_of(lists[first + k, p], 16), tokens), :] for k in range(GROUP)]
        similar = lax.dot_general(
            passages[p], jnp.concatenate(rows, axis=0), NT, preferred_element_type=jnp.float32
        )
        return jnp.max(similar.reshape(length // 8, 8, GROUP * tokens), axis=0)

    def extra_facts(e):
        live = e < extras[2, 0]
        return jnp.where(live, extras[0, e], -1), extras[0, e], extras[1, e]

    lane = lax.broadcasted_iota(jnp.int32, (GROUP, LANES), 1)
    for p in range(slots):
        best[p] = group_best(p, 0)
    if most > 1:
        for copy in copies[1:]:
            copy.wait()
        facts = [extra_facts(e) for e in range(EXTRA)]
        for e, (_, p, j) in enumerate(facts):
            best[slots + e] = group_best(p, j * GROUP)
    means = token_means(jnp.max(best[...], axis=1), tokens)
    table[0:GROUP, 0:slots] = means[:, 0:slots]
    if most > 1:
        for j in range(1, most):
            total = jnp.zeros((GROUP, LANES), jnp.float32)
            for e, (at, _, its) in enumerate(facts):
                total = jnp.where(lane == jnp.where(its == j, at, -1), means[:, slots + e : slots + e + 1], total)
            table[j * GROUP : (j + 1) * GROUP, :] = total

        def step(i, carry):
            where = [extra_facts(i * EXTRA + u) for u in range(EXTRA)]
            for u, (_, p, j) in enumerate(where):
                best[u] = group_best(p, j * GROUP)
            means = token_means(jnp.max(best[0:EXTRA], axis=1), tokens)
            for u, (at, _, j) in enumerate(where):
                rows = pl.ds(pl.multiple_of(j * GROUP, GROUP), GROUP)
                table[rows, :] = jnp.where(lane == at, means[:, u : u + 1], table[rows, :])
            return carry

        lax.fori_loop(1, lax.div(extras[2, 0] + (EXTRA - 1), EXTRA), step, 0)
    result = jnp.zeros((queries, LANES), jnp.float32)
    for r in range(queries):
        result = jnp.where(rank == r, table[r : r + 1, :], result)
    return result


def score_scratch(slots, tokens, queries):
    return [
        pltpu.VMEM((slots + EXTRA, 8, GROUP * tokens), jnp.float32),
        pltpu.VMEM((queries, LANES), jnp.float32),
        pltpu.VMEM((queries, LANES), jnp.int32),
        pltpu.SMEM((queries, LANES), jnp.int32),
        pltpu.VMEM((8, 256), jnp.int32),
        pltpu.SMEM((8, 256), jnp.int32),
        pltpu.SemaphoreType.DMA((3,)),
    ]


def cost(passages, queries):
    return pl.CostEstimate(
        flops=2 * passages.size * 256 * (queries // 4), bytes_accessed=passages.size * 2, transcendentals=0
    )


def score_kernel(block_rows, block_count, tokens, cand_count, me, passages, blocks, out, *scratch):
    out[...] = score_blocks(
        block_rows, block_count, tokens, cand_count, me[0].astype(jnp.float32), passages, blocks, *scratch
    )


def score(me, passages, blocks, block_rows, block_count, tokens, cand_count):
    queries = block_count * (REQUEST_ROWS // 2)
    return pl.pallas_call(
        functools.partial(score_kernel, block_rows, block_count, tokens, cand_count),
        out_shape=jax.ShapeDtypeStruct((queries, LANES), jnp.float32),
        in_specs=[pl.BlockSpec(memory_space=pltpu.SMEM), VMEM, VMEM],
        out_specs=VMEM,
        scratch_shapes=score_scratch(passages.shape[0], tokens, queries),
        compiler_params=params(16),
        cost_estimate=cost(passages, queries),
    )(me, passages, blocks)


def last_kernel(steps, block_rows, block_count, tokens, cand_count, me, passages, blocks, line, out, *scratch):
    per_block = REQUEST_ROWS // 2
    result = score_blocks(
        block_rows, block_count, tokens, cand_count, me[0].astype(jnp.float32), passages, blocks, *scratch
    )
    for b, step in enumerate(steps):
        rows = slice(b * per_block, (b + 1) * per_block)
        out[jnp.bitwise_xor(me[0], step)] = line[rows, :]
        out[jnp.bitwise_xor(me[0], step + 1)] = result[rows, :]


def score_last(me, passages, blocks, line, steps, block_rows, block_count, tokens, cand_count):
    per_block = REQUEST_ROWS // 2
    return pl.pallas_call(
        functools.partial(last_kernel, steps, block_rows, block_count, tokens, cand_count),
        out_shape=jax.ShapeDtypeStruct((2 * block_count, per_block, LANES), jnp.float32),
        in_specs=[pl.BlockSpec(memory_space=pltpu.SMEM), VMEM, VMEM, VMEM],
        out_specs=VMEM,
        scratch_shapes=score_scratch(passages.shape[0], tokens, block_count * per_block),
        compiler_params=params(16),
        cost_estimate=cost(passages, block_count * per_block),
    )(me, passages, blocks, line)


def select_kernel(returned, owner, slot, out):
    count = owner.shape[1]
    own, at = wide(owner[...], -1), wide(slot[...], 0)
    total = jnp.zeros(own.shape, jnp.float32)
    for s in range(returned.shape[0]):
        total = jnp.where(own == s, jnp.take_along_axis(returned[s], at, axis=1, mode="promise_in_bounds"), total)
    out[...] = total[:, :count]


def select(returned, owner, slot):
    return pl.pallas_call(
        select_kernel,
        out_shape=jax.ShapeDtypeStruct(owner.shape, jnp.float32),
        in_specs=[VMEM] * 3,
        out_specs=VMEM,
        compiler_params=params(4),
    )(returned, owner, slot)


def local(queries, passages, lengths, token_mask, cand_owner, cand_slot):
    shard_count = lax.axis_size("shard")
    query_count, tokens, dim = queries.shape
    cand_count = cand_owner.shape[1]
    block = pack(queries.reshape(query_count * tokens, dim), cand_owner, cand_slot)
    block_rows = block.shape[0]
    filled = fill(passages, lengths, token_mask)
    me = lax.axis_index("shard").reshape(1)
    sizes = dict(block_rows=block_rows, block_count=4, tokens=tokens, cand_count=cand_count)
    if shard_count == 8:
        swap = lambda x, d: lax.ppermute(x, "shard", [(i, i ^ d) for i in range(shard_count)])
        far, mid, near = swap(block, 4), swap(block, 6), swap(block, 2)
        line = jnp.concatenate([block, near, far, mid], axis=0)
        other = swap(line, 1)
        line_scores = score(me, filled, line, **sizes)
        by_home = score_last(me, filled, other, line_scores, steps=(0, 2, 4, 6), **sizes)
    else:
        every = lax.all_gather(block, "shard", axis=0, tiled=True)
        parts = every.reshape(shard_count // 4, 4 * block_rows, dim)
        by_home = lax.map(lambda part: score(me, filled, part, **sizes), parts)
        by_home = by_home.reshape(shard_count, query_count, LANES)
    returned = lax.all_to_all(by_home, "shard", split_axis=0, concat_axis=0, tiled=True)
    return select(returned, cand_owner, cand_slot)


def solution(mesh):
    in_specs = (
        P(("groups", "shard", "rep"), None, None),
        P(("groups", "shard"), None, None),
        P(("groups", "shard")),
        P(("groups", "shard"), None),
        P(("groups", "shard", "rep"), None),
        P(("groups", "shard", "rep"), None),
    )
    out_specs = P(("groups", "shard", "rep"), None)
    return jax.shard_map(local, mesh=mesh, in_specs=in_specs, out_specs=out_specs, check_vma=False)
```

time: 45.2 us -> 35.6 us (0.79)
  local copies, waits for them, and re-layouts: 7.38 us -> 0.01 us
  waiting for transfers between devices: 0.05 us -> 4.4 us
  Pallas kernels: 17 us -> 13.3 us
  blocking collectives: 12.1 us -> 10.4 us
  other arithmetic: 0.75 us -> 0.02 us
    unnamed x10 -> x4, local copies, waits for them, and re-layouts: 4.98 us -> 0.01 us
    ppermute x4, waiting for transfers between devices: 0.05 us -> 4.4 us  [local(): lax.ppermute(x, 'shard', [(i, i ^ d) for i in range(shard_count)])]
    pallas_call x3 -> x4, Pallas kernels: 15.5 us -> 12.6 us  [the longest x1 4.27 us: score_last(): pl.pallas_call(functools.partial(last_kernel, steps, block_rows, block_co...]
    gather x2 -> x0, local copies, waits for them, and re-layouts: 1.88 us -> none  [local(): by_dest = by_step[place[jnp.arange(8) ^ me]]]
    all_to_all x1, blocking collectives: 12.1 us -> 10.4 us  [local(): lax.all_to_all(by_home, 'shard', split_axis=0, concat_axis=0, tiled=True)]
    pallas_call x1, Pallas kernels: 1.52 us -> 0.67 us  [select(): pl.pallas_call(select_kernel, out_shape=jax.ShapeDtypeStruct(owner.shape,...]
    all_to_all x1 -> x0, other arithmetic: 0.68 us -> none  [local(): lax.all_to_all(by_dest, 'shard', split_axis=0, concat_axis=0, tiled=True)]
    all_to_all x1 -> x0, local copies, waits for them, and re-layouts: 0.51 us -> none  [local(): lax.all_to_all(by_dest, 'shard', split_axis=0, concat_axis=0, tiled=True)]
  transfers between devices with their start and end apart: 4 -> 4, of which waited for: 0 -> 2; matrix products, arithmetic and copies ran while one was open for 3% -> 0% of each run, Pallas kernels for 17% -> 21%
where the time goes in v2:
time: 35.6 us; the launch traced here: 35.4 us
  Pallas kernels  13.3 us (37%)
  blocking collectives  10.4 us (29%)
  starting transfers between devices  7.31 us (21%)
  waiting for transfers between devices  4.4 us (12%)
    all_to_all x1, blocking collectives, local(): lax.all_to_all(by_home, 'shard', split_axis=0, concat_axis=0, tiled=True)  10.4 us
    ppermute x4, starting transfers between devices, local(): lax.ppermute(x, 'shard', [(i, i ^ d) for i in range(shard_count)])  7.31 us
    ppermute x4, waiting for transfers between devices, local(): lax.ppermute(x, 'shard', [(i, i ^ d) for i in range(shard_count)])  4.4 us
    pallas_call x1, Pallas kernels, score_last(): pl.pallas_call(functools.partial(last_kernel, steps, block_rows, block_co...  4.27 us
    pallas_call x1, Pallas kernels, score(): pl.pallas_call(functools.partial(score_kernel, block_rows, block_count, t...  4.26 us
    pallas_call x1, Pallas kernels, fill(): pl.pallas_call(fill_kernel, out_shape=pltpu.VMEM(passages.shape, jnp.bflo...  3.19 us
    pallas_call x1, Pallas kernels, pack(): pl.pallas_call(pack_kernel, out_shape=pltpu.VMEM((rows.shape[0] + REQUEST...  0.86 us
  transfers between devices with their start and end apart: 4, of which 2 were waited for; matrix products, arithmetic and copies ran while one was open for 0% of the time, Pallas kernels for 21%

profile of v2, /device:TPU:0, one launch (start us, length us, event | category | flops | bytes accessed | tf_op | source)
XLA Modules:
  0.0 35.4 jit_solution(6888824883905439478)
XLA Ops:
  0.0 0.9 %shard_map.65 = bf16[272,128]{1,0:T(8,128)(2,1)S(1)} custom-call(bf16[256,128]{1,0:T(8,128)(2,1)} %bitcast.2, s32[8,100]{1,0:T(8,128)} %owner.3, s32[8,100]{1,0:T(8,128)} %slot.3), custom_call_target="tpu_custom_call" | custom-call | tf_op jit(solution)/shard_map/pallas_call | solution.py:48
  0.9 5.1 %collective-permute-start.2 = (bf16[272,128]{1,0:T(8,128)(2,1)S(1)}, bf16[272,128]{1,0:T(8,128)(2,1)S(1)}, u32[]{:S(2)}, u32[]{:S(2)}) collective-permute-start(bf16[272,128]{1,0:T(8,128)(2,1)S(1)} %shard_map.65), channel_id=1, source_target_pairs={{0,12},{2,14},{4,8},{6,10},{8,4},{10,6},{12,0},{14,2},{1,13},{3,15... | collective-permute-start | bytes 208904 | tf_op jit(solution)/shard_map/ppermute | solution.py:326
  6.0 0.0 collective-permute-start.1
  6.0 0.6 %collective-permute-start = (bf16[272,128]{1,0:T(8,128)(2,1)S(1)}, bf16[272,128]{1,0:T(8,128)(2,1)S(1)}, u32[]{:S(2)}, u32[]{:S(2)}) collective-permute-start(bf16[272,128]{1,0:T(8,128)(2,1)S(1)} %shard_map.65), channel_id=1, source_target_pairs={{0,4},{2,6},{4,0},{6,2},{8,12},{10,14},{12,8},{14,10},{1,5},{3,7},... | collective-permute-start | bytes 208904 | tf_op jit(solution)/shard_map/ppermute | solution.py:326
  6.6 3.2 %shard_map.64.passages = bf16[64,192,128]{2,1,0:T(8,128)(2,1)S(1)} custom-call(bf16[64,192,128]{2,1,0:T(8,128)(2,1)} %passages.1, s32[64]{0:T(128)} %lengths.1, s32[64,192]{1,0:T(8,128)} %mask.1), custom_call_target="tpu_custom_call" | custom-call | bytes 6291456 | tf_op jit(solution)/shard_map/pallas_call | solution.py:94
  9.8 0.0 collective-permute-done.2
  9.8 2.1 %collective-permute-done.1 = bf16[272,128]{1,0:T(8,128)(2,1)S(1)} collective-permute-done((bf16[272,128]{1,0:T(8,128)(2,1)S(1)}, bf16[272,128]{1,0:T(8,128)(2,1)S(1)}, u32[]{:S(2)}, u32[]{:S(2)}) %collective-permute-start.1) | collective-permute-done | bytes 69664 | tf_op jit(solution)/shard_map/ppermute | solution.py:326
  11.9 0.0 collective-permute-done
  11.9 1.6 %collective-permute-start.3 = (bf16[1088,128]{1,0:T(8,128)(2,1)S(1)}, bf16[1088,128]{1,0:T(8,128)(2,1)S(1)}, u32[]{:S(2)}, u32[]{:S(2)}) collective-permute-start(bf16[1088,128]{1,0:T(8,128)(2,1)S(1)} %pad_maximum_fusion.blocks), channel_id=1, source_target_pairs={{0,2},{2,0},{4,6},{6,4},{8,10},{10,8},{12,14},{14,12},{1,3},{3,1},... | collective-permute-start | bytes 835592 | tf_op jit(solution)/shard_map/ppermute | solution.py:326
  13.5 4.3 %shard_map.66.line = f32[32,128]{1,0:T(8,128)S(1)} custom-call(s32[1]{0:T(128)} %bitcast.me, bf16[64,192,128]{2,1,0:T(8,128)(2,1)S(1)} %shard_map.64.passages, bf16[1088,128]{1,0:T(8,128)(2,1)S(1)} %pad_maximum_fusion.blocks), custom_call_target="tpu_custom_call" | custom-call | flops 6442450944 | bytes 3145728 | tf_op jit(solution)/shard_map/pallas_call | solution.py:262
  17.7 0.0 copy-start
  17.8 0.0 copy-start.1
  17.8 2.3 %collective-permute-done.3.blocks = bf16[1088,128]{1,0:T(8,128)(2,1)S(1)} collective-permute-done((bf16[1088,128]{1,0:T(8,128)(2,1)S(1)}, bf16[1088,128]{1,0:T(8,128)(2,1)S(1)}, u32[]{:S(2)}, u32[]{:S(2)}) %collective-permute-start.3) | collective-permute-done | bytes 278560 | tf_op jit(solution)/shard_map/ppermute | solution.py:326
  20.1 4.3 %shard_map.67 = f32[8,8,128]{2,1,0:T(8,128)S(1)} custom-call(s32[1]{0:T(128)} %bitcast.me, bf16[64,192,128]{2,1,0:T(8,128)(2,1)S(1)} %shard_map.64.passages, bf16[1088,128]{1,0:T(8,128)(2,1)S(1)} %collective-permute-done.3.blocks, f32[32,128]{1,0:T(8,128)S(1)} %shard_map.66.line), custom_call_target="tpu_custom_call" | custom-call | flops 6442450944 | bytes 3145728 | tf_op jit(solution)/shard_map/pallas_call | solution.py:286
  24.4 10.4 %all_to_all.5.returned = f32[8,8,128]{2,1,0:T(8,128)S(1)} all-to-all(f32[8,8,128]{2,1,0:T(8,128)S(1)} %shard_map.67), channel_id=1, replica_groups=mesh['groups'=2,'shard'=8,'rep'=2] {'shard'}, dimensions={0} | all-to-all | bytes 65536 | tf_op jit(solution)/shard_map/all_to_all | solution.py:337
  34.7 0.0 copy-done
  34.7 0.0 copy-done.1
  34.7 0.7 %shard_map.68 = f32[8,100]{1,0:T(8,128)} custom-call(f32[8,8,128]{2,1,0:T(8,128)S(1)} %all_to_all.5.returned, s32[8,100]{1,0:T(8,128)S(1)} %copy-done, s32[8,100]{1,0:T(8,128)S(1)} %copy-done.1), custom_call_target="tpu_custom_call" | custom-call | tf_op jit(solution)/shard_map/pallas_call | solution.py:307
  (1 shorter events, 0.0 us)
Async XLA Ops:
  0.9 9.0 %collective-permute-start.2 = (bf16[272,128]{1,0:T(8,128)(2,1)S(1)}, bf16[272,128]{1,0:T(8,128)(2,1)S(1)}, u32[]{:S(2)}, u32[]{:S(2)}) collective-permute-start(bf16[272,128]{1,0:T(8,128)(2,1)S(1)} %shard_map.65), channel_id=1, source_target_pairs={{0,12},{2,14},{4,8},{6,10},{8,4},{10,6},{12,0},{14,2},{1,13},{3,15... | collective-permute-start | bytes 208904 | tf_op jit(solution)/shard_map/ppermute | solution.py:326
  6.0 5.9 %collective-permute-start.1 = (bf16[272,128]{1,0:T(8,128)(2,1)S(1)}, bf16[272,128]{1,0:T(8,128)(2,1)S(1)}, u32[]{:S(2)}, u32[]{:S(2)}) collective-permute-start(bf16[272,128]{1,0:T(8,128)(2,1)S(1)} %shard_map.65), channel_id=1, source_target_pairs={{0,8},{2,10},{4,12},{6,14},{8,0},{10,2},{12,4},{14,6},{1,9},{3,11}... | collective-permute-start | bytes 208904 | tf_op jit(solution)/shard_map/ppermute | solution.py:326
  6.0 5.9 %collective-permute-start = (bf16[272,128]{1,0:T(8,128)(2,1)S(1)}, bf16[272,128]{1,0:T(8,128)(2,1)S(1)}, u32[]{:S(2)}, u32[]{:S(2)}) collective-permute-start(bf16[272,128]{1,0:T(8,128)(2,1)S(1)} %shard_map.65), channel_id=1, source_target_pairs={{0,4},{2,6},{4,0},{6,2},{8,12},{10,14},{12,8},{14,10},{1,5},{3,7},... | collective-permute-start | bytes 208904 | tf_op jit(solution)/shard_map/ppermute | solution.py:326
  11.9 8.2 %collective-permute-start.3 = (bf16[1088,128]{1,0:T(8,128)(2,1)S(1)}, bf16[1088,128]{1,0:T(8,128)(2,1)S(1)}, u32[]{:S(2)}, u32[]{:S(2)}) collective-permute-start(bf16[1088,128]{1,0:T(8,128)(2,1)S(1)} %pad_maximum_fusion.blocks), channel_id=1, source_target_pairs={{0,2},{2,0},{4,6},{6,4},{8,10},{10,8},{12,14},{14,12},{1,3},{3,1},... | collective-permute-start | bytes 835592 | tf_op jit(solution)/shard_map/ppermute | solution.py:326
  17.7 17.0 %copy-start = (s32[8,100]{1,0:T(8,128)S(1)}, s32[8,100]{1,0:T(8,128)}, u32[]{:S(2)}) copy-start(s32[8,100]{1,0:T(8,128)} %owner.3) | copy-start | bytes 9604
  17.8 17.0 %copy-start.1 = (s32[8,100]{1,0:T(8,128)S(1)}, s32[8,100]{1,0:T(8,128)}, u32[]{:S(2)}) copy-start(s32[8,100]{1,0:T(8,128)} %slot.3) | copy-start | bytes 9604

commit v3 on v2

--- a/solution.py
+++ b/solution.py
@@ -11,7 +11,7 @@
 LANES = 128
 GROUP = 8
 REQUEST_ROWS = 16
-EXTRA = 16
+EXTRA = 12
 VMEM = pl.BlockSpec(memory_space=pltpu.VMEM)
 HBM = pl.BlockSpec(memory_space=pltpu.HBM)
 
@@ -61,7 +61,7 @@
 
 def fill_kernel(passages, lengths, mask, out, mask_here, lengths_here, sems):
     slots, tokens, _ = passages.shape
-    parts = 8
+    parts = 4
     each = slots // parts
     head = [
         pltpu.make_async_copy(mask, mask_here, sems.at[parts]),
@@ -78,16 +78,13 @@
     positions = lax.broadcasted_iota(jnp.int32, (tokens, slots), 0)
     taken = mask_here[...].astype(jnp.float32).T > 0.5
     valid = (positions < lengths_here[...].reshape(1, slots)) & (taken | (positions == 0))
-    valid = wide(jnp.where(valid, 1.0, 0.0), 0.0).astype(jnp.bfloat16)
-    lane = lax.broadcasted_iota(jnp.int32, (tokens, LANES), 1)
-    ones = jnp.ones((LANES, LANES), jnp.bfloat16)
+    valid = wide(jnp.where(valid, 1.0, 0.0), 0.0)
     for i in range(parts):
         copies[i].wait()
         for p in range(i * each, (i + 1) * each):
-            one = jnp.where(lane == p, valid, 0).astype(jnp.bfloat16)
-            keep = jnp.dot(one, ones, preferred_element_type=jnp.float32) > 0.5
-            tok = out[p].astype(jnp.float32)
-            out[p] = jnp.where(keep, tok, tok[0:1]).astype(jnp.bfloat16)
+            keep = jnp.broadcast_to(valid[:, p : p + 1], (tokens, LANES)).astype(jnp.bfloat16) > 0.5
+            tok = out[p]
+            out[p] = jnp.where(keep, tok, tok[0:1])
 
 
 def fill(passages, lengths, mask):
@@ -277,8 +274,9 @@
     )
     for b, step in enumerate(steps):
         rows = slice(b * per_block, (b + 1) * per_block)
-        out[jnp.bitwise_xor(me[0], step)] = line[rows, :]
-        out[jnp.bitwise_xor(me[0], step + 1)] = result[rows, :]
+        home = lax.rem(me[0] + (2 * len(steps) - step), 2 * len(steps))
+        out[home] = line[rows, :]
+        out[jnp.bitwise_xor(home, 1)] = result[rows, :]
 
 
 def score_last(me, passages, blocks, line, steps, block_rows, block_count, tokens, cand_count):
@@ -324,11 +322,17 @@
     sizes = dict(block_rows=block_rows, block_count=4, tokens=tokens, cand_count=cand_count)
     if shard_count == 8:
         swap = lambda x, d: lax.ppermute(x, "shard", [(i, i ^ d) for i in range(shard_count)])
-        far, mid, near = swap(block, 4), swap(block, 6), swap(block, 2)
+        turn = lambda x, d: lax.ppermute(x, "shard", [(i, (i + d) % shard_count) for i in range(shard_count)])
+        near, far, mid = turn(block, 6), turn(block, 4), turn(block, 2)
+        own = swap(block, 1)
+        near, filled = lax.optimization_barrier((near, filled))
+        first = swap(near, 1)
+        far, mid, near = lax.optimization_barrier((far, mid, near))
+        second = swap(jnp.concatenate([far, mid], axis=0), 1)
         line = jnp.concatenate([block, near, far, mid], axis=0)
-        other = swap(line, 1)
+        other = jnp.concatenate([own, first, second], axis=0)
         line_scores = score(me, filled, line, **sizes)
-        by_home = score_last(me, filled, other, line_scores, steps=(0, 2, 4, 6), **sizes)
+        by_home = score_last(me, filled, other, line_scores, steps=(0, 6, 4, 2), **sizes)
     else:
         every = lax.all_gather(block, "shard", axis=0, tiled=True)
         parts = every.reshape(shard_count // 4, 4 * block_rows, dim)

time: 35.6 us -> 33.5 us (0.941)
  waiting for transfers between devices: 4.4 us -> 1.2 us
  starting transfers between devices: 7.31 us -> 9.76 us
  Pallas kernels: 13.3 us -> 12.3 us
  blocking collectives: 10.4 us -> 9.94 us
    ppermute x0 -> x3, starting transfers between devices: none -> 6.11 us  [local(): lax.ppermute(x, 'shard', [(i, (i + d) % shard_count) for i in range(shard...]
    ppermute x4 -> x3, waiting for transfers between devices: 4.4 us -> 0.01 us  [local(): lax.ppermute(x, 'shard', [(i, i ^ d) for i in range(shard_count)])]
    ppermute x4 -> x3, starting transfers between devices: 7.31 us -> 3.65 us  [local(): lax.ppermute(x, 'shard', [(i, i ^ d) for i in range(shard_count)])]
    ppermute x0 -> x3, waiting for transfers between devices: none -> 1.2 us  [local(): lax.ppermute(x, 'shard', [(i, (i + d) % shard_count) for i in range(shard...]
    pallas_call x1, Pallas kernels: 3.19 us -> 2.46 us  [fill(): pl.pallas_call(fill_kernel, out_shape=pltpu.VMEM(passages.shape, jnp.bflo...]
    all_to_all x1, blocking collectives: 10.4 us -> 9.94 us  [local(): lax.all_to_all(by_home, 'shard', split_axis=0, concat_axis=0, tiled=True)]
  transfers between devices with their start and end apart: 4 -> 6, of which waited for: 2 -> 1; matrix products, arithmetic and copies ran while one was open for 0% -> 0% of each run, Pallas kernels for 21% -> 20%
where the time goes in v3:
time: 33.5 us; the launch traced here: 33.3 us
  Pallas kernels  12.3 us (37%)
  blocking collectives  9.94 us (30%)
  starting transfers between devices  9.76 us (29%)
  waiting for transfers between devices  1.2 us (4%)
    all_to_all x1, blocking collectives, local(): lax.all_to_all(by_home, 'shard', split_axis=0, concat_axis=0, tiled=True)  9.94 us
    ppermute x3, starting transfers between devices, local(): lax.ppermute(x, 'shard', [(i, (i + d) % shard_count) for i in range(shard...  6.11 us
    pallas_call x1, Pallas kernels, score_last(): pl.pallas_call(functools.partial(last_kernel, steps, block_rows, block_co...  4.13 us
    pallas_call x1, Pallas kernels, score(): pl.pallas_call(functools.partial(score_kernel, block_rows, block_count, t...  4.13 us
    ppermute x3, starting transfers between devices, local(): lax.ppermute(x, 'shard', [(i, i ^ d) for i in range(shard_count)])  3.65 us
    pallas_call x1, Pallas kernels, fill(): pl.pallas_call(fill_kernel, out_shape=pltpu.VMEM(passages.shape, jnp.bflo...  2.46 us
    ppermute x3, waiting for transfers between devices, local(): lax.ppermute(x, 'shard', [(i, (i + d) % shard_count) for i in range(shard...  1.2 us
    pallas_call x1, Pallas kernels, pack(): pl.pallas_call(pack_kernel, out_shape=pltpu.VMEM((rows.shape[0] + REQUEST...  0.86 us
  transfers between devices with their start and end apart: 6, of which 1 were waited for; matrix products, arithmetic and copies ran while one was open for 0% of the time, Pallas kernels for 20%

profile of v3, /device:TPU:0, one launch (start us, length us, event | category | flops | bytes accessed | tf_op | source)
XLA Modules:
  0.0 33.3 jit_solution(9985522135588936140)
XLA Ops:
  0.0 0.9 %shard_map.64 = bf16[272,128]{1,0:T(8,128)(2,1)S(1)} custom-call(bf16[256,128]{1,0:T(8,128)(2,1)} %bitcast.2, s32[8,100]{1,0:T(8,128)} %owner.3, s32[8,100]{1,0:T(8,128)} %slot.3), custom_call_target="tpu_custom_call" | custom-call | tf_op jit(solution)/shard_map/pallas_call | solution.py:48
  0.9 5.1 %collective-permute-start = (bf16[272,128]{1,0:T(8,128)(2,1)S(1)}, bf16[272,128]{1,0:T(8,128)(2,1)S(1)}, u32[]{:S(2)}, u32[]{:S(2)}) collective-permute-start(bf16[272,128]{1,0:T(8,128)(2,1)S(1)} %shard_map.64), channel_id=1, source_target_pairs={{0,12},{2,14},{4,0},{6,2},{8,4},{10,6},{12,8},{14,10},{1,13},{3,15... | collective-permute-start | bytes 208904 | tf_op jit(solution)/shard_map/ppermute | solution.py:325
  6.0 0.0 collective-permute-start.3
  6.0 1.0 %collective-permute-start.4 = (bf16[272,128]{1,0:T(8,128)(2,1)S(1)}, bf16[272,128]{1,0:T(8,128)(2,1)S(1)}, u32[]{:S(2)}, u32[]{:S(2)}) collective-permute-start(bf16[272,128]{1,0:T(8,128)(2,1)S(1)} %shard_map.64), channel_id=1, source_target_pairs={{0,4},{2,6},{4,8},{6,10},{8,12},{10,14},{12,0},{14,2},{1,5},{3,7},... | collective-permute-start | bytes 208904 | tf_op jit(solution)/shard_map/ppermute | solution.py:325
  7.0 1.5 %collective-permute-start.1 = (bf16[272,128]{1,0:T(8,128)(2,1)S(1)}, bf16[272,128]{1,0:T(8,128)(2,1)S(1)}, u32[]{:S(2)}, u32[]{:S(2)}) collective-permute-start(bf16[272,128]{1,0:T(8,128)(2,1)S(1)} %shard_map.64), channel_id=1, source_target_pairs={{0,2},{2,0},{4,6},{6,4},{8,10},{10,8},{12,14},{14,12},{1,3},{3,1},... | collective-permute-start | bytes 208904 | tf_op jit(solution)/shard_map/ppermute | solution.py:324
  8.5 2.5 %shard_map.65.passages = bf16[64,192,128]{2,1,0:T(8,128)(2,1)S(1)} custom-call(bf16[64,192,128]{2,1,0:T(8,128)(2,1)} %passages.1, s32[64]{0:T(128)} %lengths.1, s32[64,192]{1,0:T(8,128)} %mask.1), custom_call_target="tpu_custom_call" | custom-call | bytes 6291456 | tf_op jit(solution)/shard_map/pallas_call | solution.py:91
  10.9 0.0 collective-permute-done
  11.0 0.6 %collective-permute-start.2 = (bf16[272,128]{1,0:T(8,128)(2,1)S(1)}, bf16[272,128]{1,0:T(8,128)(2,1)S(1)}, u32[]{:S(2)}, u32[]{:S(2)}) collective-permute-start(bf16[272,128]{1,0:T(8,128)(2,1)S(1)} %collective-permute-done), channel_id=1, source_target_pairs={{0,2},{2,0},{4,6},{6,4},{8,10},{10,8},{12,14},{14,12},{1,3},{3,1},... | collective-permute-start | bytes 208904 | tf_op jit(solution)/shard_map/ppermute | solution.py:324
  11.6 1.2 %collective-permute-done.3 = bf16[272,128]{1,0:T(8,128)(2,1)S(1)} collective-permute-done((bf16[272,128]{1,0:T(8,128)(2,1)S(1)}, bf16[272,128]{1,0:T(8,128)(2,1)S(1)}, u32[]{:S(2)}, u32[]{:S(2)}) %collective-permute-start.3) | collective-permute-done | bytes 69664 | tf_op jit(solution)/shard_map/ppermute | solution.py:325
  12.8 0.0 collective-permute-done.4
  12.8 1.6 %collective-permute-start.5 = (bf16[544,128]{1,0:T(8,128)(2,1)S(1)}, bf16[544,128]{1,0:T(8,128)(2,1)S(1)}, u32[]{:S(2)}, u32[]{:S(2)}) collective-permute-start(bf16[544,128]{1,0:T(8,128)(2,1)S(1)} %pad_maximum_fusion.2), channel_id=1, source_target_pairs={{0,2},{2,0},{4,6},{6,4},{8,10},{10,8},{12,14},{14,12},{1,3},{3,1},... | collective-permute-start | bytes 417800 | tf_op jit(solution)/shard_map/ppermute | solution.py:324
  14.4 4.1 %shard_map.66.line = f32[32,128]{1,0:T(8,128)S(1)} custom-call(s32[1]{0:T(128)} %bitcast.me, bf16[64,192,128]{2,1,0:T(8,128)(2,1)S(1)} %shard_map.65.passages, bf16[1088,128]{1,0:T(8,128)(2,1)S(1)} %pad_maximum_fusion.1.blocks), custom_call_target="tpu_custom_call" | custom-call | flops 6442450944 | bytes 3145728 | tf_op jit(solution)/shard_map/pallas_call | solution.py:259
  18.5 0.0 collective-permute-done.1
  18.5 0.0 collective-permute-done.2
  18.5 0.0 collective-permute-done.5
  18.6 0.0 copy-start
  18.6 0.0 copy-start.1
  18.6 4.1 %shard_map.67 = f32[8,8,128]{2,1,0:T(8,128)S(1)} custom-call(s32[1]{0:T(128)} %bitcast.me, bf16[64,192,128]{2,1,0:T(8,128)(2,1)S(1)} %shard_map.65.passages, bf16[1088,128]{1,0:T(8,128)(2,1)S(1)} %pad_maximum_fusion.blocks, f32[32,128]{1,0:T(8,128)S(1)} %shard_map.66.line), custom_call_target="tpu_custom_call" | custom-call | flops 6442450944 | bytes 3145728 | tf_op jit(solution)/shard_map/pallas_call | solution.py:284
  22.7 9.9 %all_to_all.5.returned = f32[8,8,128]{2,1,0:T(8,128)S(1)} all-to-all(f32[8,8,128]{2,1,0:T(8,128)S(1)} %shard_map.67), channel_id=1, replica_groups=mesh['groups'=2,'shard'=8,'rep'=2] {'shard'}, dimensions={0} | all-to-all | bytes 65536 | tf_op jit(solution)/shard_map/all_to_all | solution.py:341
  32.7 0.0 copy-done
  32.7 0.0 copy-done.1
  32.7 0.7 %shard_map.68 = f32[8,100]{1,0:T(8,128)} custom-call(f32[8,8,128]{2,1,0:T(8,128)S(1)} %all_to_all.5.returned, s32[8,100]{1,0:T(8,128)S(1)} %copy-done, s32[8,100]{1,0:T(8,128)S(1)} %copy-done.1), custom_call_target="tpu_custom_call" | custom-call | tf_op jit(solution)/shard_map/pallas_call | solution.py:305
  (3 shorter events, 0.1 us)
Async XLA Ops:
  0.9 10.1 %collective-permute-start = (bf16[272,128]{1,0:T(8,128)(2,1)S(1)}, bf16[272,128]{1,0:T(8,128)(2,1)S(1)}, u32[]{:S(2)}, u32[]{:S(2)}) collective-permute-start(bf16[272,128]{1,0:T(8,128)(2,1)S(1)} %shard_map.64), channel_id=1, source_target_pairs={{0,12},{2,14},{4,0},{6,2},{8,4},{10,6},{12,8},{14,10},{1,13},{3,15... | collective-permute-start | bytes 208904 | tf_op jit(solution)/shard_map/ppermute | solution.py:325
  6.0 6.8 %collective-permute-start.3 = (bf16[272,128]{1,0:T(8,128)(2,1)S(1)}, bf16[272,128]{1,0:T(8,128)(2,1)S(1)}, u32[]{:S(2)}, u32[]{:S(2)}) collective-permute-start(bf16[272,128]{1,0:T(8,128)(2,1)S(1)} %shard_map.64), channel_id=1, source_target_pairs={{0,8},{2,10},{4,12},{6,14},{8,0},{10,2},{12,4},{14,6},{1,9},{3,11}... | collective-permute-start | bytes 208904 | tf_op jit(solution)/shard_map/ppermute | solution.py:325
  6.0 6.8 %collective-permute-start.4 = (bf16[272,128]{1,0:T(8,128)(2,1)S(1)}, bf16[272,128]{1,0:T(8,128)(2,1)S(1)}, u32[]{:S(2)}, u32[]{:S(2)}) collective-permute-start(bf16[272,128]{1,0:T(8,128)(2,1)S(1)} %shard_map.64), channel_id=1, source_target_pairs={{0,4},{2,6},{4,8},{6,10},{8,12},{10,14},{12,0},{14,2},{1,5},{3,7},... | collective-permute-start | bytes 208904 | tf_op jit(solution)/shard_map/ppermute | solution.py:325
  7.0 11.5 %collective-permute-start.1 = (bf16[272,128]{1,0:T(8,128)(2,1)S(1)}, bf16[272,128]{1,0:T(8,128)(2,1)S(1)}, u32[]{:S(2)}, u32[]{:S(2)}) collective-permute-start(bf16[272,128]{1,0:T(8,128)(2,1)S(1)} %shard_map.64), channel_id=1, source_target_pairs={{0,2},{2,0},{4,6},{6,4},{8,10},{10,8},{12,14},{14,12},{1,3},{3,1},... | collective-permute-start | bytes 208904 | tf_op jit(solution)/shard_map/ppermute | solution.py:324
  11.0 7.5 %collective-permute-start.2 = (bf16[272,128]{1,0:T(8,128)(2,1)S(1)}, bf16[272,128]{1,0:T(8,128)(2,1)S(1)}, u32[]{:S(2)}, u32[]{:S(2)}) collective-permute-start(bf16[272,128]{1,0:T(8,128)(2,1)S(1)} %collective-permute-done), channel_id=1, source_target_pairs={{0,2},{2,0},{4,6},{6,4},{8,10},{10,8},{12,14},{14,12},{1,3},{3,1},... | collective-permute-start | bytes 208904 | tf_op jit(solution)/shard_map/ppermute | solution.py:324
  12.8 5.7 %collective-permute-start.5 = (bf16[544,128]{1,0:T(8,128)(2,1)S(1)}, bf16[544,128]{1,0:T(8,128)(2,1)S(1)}, u32[]{:S(2)}, u32[]{:S(2)}) collective-permute-start(bf16[544,128]{1,0:T(8,128)(2,1)S(1)} %pad_maximum_fusion.2), channel_id=1, source_target_pairs={{0,2},{2,0},{4,6},{6,4},{8,10},{10,8},{12,14},{14,12},{1,3},{3,1},... | collective-permute-start | bytes 417800 | tf_op jit(solution)/shard_map/ppermute | solution.py:324
  18.6 14.1 %copy-start = (s32[8,100]{1,0:T(8,128)S(1)}, s32[8,100]{1,0:T(8,128)}, u32[]{:S(2)}) copy-start(s32[8,100]{1,0:T(8,128)} %owner.3) | copy-start | bytes 9604
  18.6 14.1 %copy-start.1 = (s32[8,100]{1,0:T(8,128)S(1)}, s32[8,100]{1,0:T(8,128)}, u32[]{:S(2)}) copy-start(s32[8,100]{1,0:T(8,128)} %slot.3) | copy-start | bytes 9604

commit v4 on v3

--- a/solution.py
+++ b/solution.py
@@ -11,7 +11,7 @@
 LANES = 128
 GROUP = 8
 REQUEST_ROWS = 16
-EXTRA = 12
+EARLY = 24
 VMEM = pl.BlockSpec(memory_space=pltpu.VMEM)
 HBM = pl.BlockSpec(memory_space=pltpu.HBM)
 
@@ -164,7 +164,7 @@
 
 
 def score_blocks(
-    block_rows, block_count, tokens, cand_count, me, passages, blocks,
+    block_rows, block_count, extra, tokens, cand_count, me, passages, blocks,
     best, table, lists_here, lists, extras_here, extras, sems,
 ):
     slots, length, dim = passages.shape
@@ -197,42 +197,43 @@
 
     lane = lax.broadcasted_iota(jnp.int32, (GROUP, LANES), 1)
     for p in range(slots):
+        if p == EARLY:
+            for copy in copies[1:]:
+                copy.wait()
         best[p] = group_best(p, 0)
     if most > 1:
-        for copy in copies[1:]:
-            copy.wait()
-        facts = [extra_facts(e) for e in range(EXTRA)]
+        facts = [extra_facts(e) for e in range(extra)]
         for e, (_, p, j) in enumerate(facts):
             best[slots + e] = group_best(p, j * GROUP)
-    means = token_means(jnp.max(best[...], axis=1), tokens)
-    table[0:GROUP, 0:slots] = means[:, 0:slots]
+    table[0:GROUP, 0:slots] = token_means(jnp.max(best[0:slots], axis=1), tokens)
+    means = token_means(jnp.max(best[slots:], axis=1), tokens)
     if most > 1:
         for j in range(1, most):
             total = jnp.zeros((GROUP, LANES), jnp.float32)
             for e, (at, _, its) in enumerate(facts):
-                total = jnp.where(lane == jnp.where(its == j, at, -1), means[:, slots + e : slots + e + 1], total)
+                total = jnp.where(lane == jnp.where(its == j, at, -1), means[:, e : e + 1], total)
             table[j * GROUP : (j + 1) * GROUP, :] = total
 
         def step(i, carry):
-            where = [extra_facts(i * EXTRA + u) for u in range(EXTRA)]
+            where = [extra_facts(i * extra + u) for u in range(extra)]
             for u, (_, p, j) in enumerate(where):
                 best[u] = group_best(p, j * GROUP)
-            means = token_means(jnp.max(best[0:EXTRA], axis=1), tokens)
+            means = token_means(jnp.max(best[0:extra], axis=1), tokens)
             for u, (at, _, j) in enumerate(where):
                 rows = pl.ds(pl.multiple_of(j * GROUP, GROUP), GROUP)
                 table[rows, :] = jnp.where(lane == at, means[:, u : u + 1], table[rows, :])
             return carry
 
-        lax.fori_loop(1, lax.div(extras[2, 0] + (EXTRA - 1), EXTRA), step, 0)
+        lax.fori_loop(1, lax.div(extras[2, 0] + (extra - 1), extra), step, 0)
     result = jnp.zeros((queries, LANES), jnp.float32)
     for r in range(queries):
         result = jnp.where(rank == r, table[r : r + 1, :], result)
     return result
 
 
-def score_scratch(slots, tokens, queries):
+def score_scratch(slots, tokens, queries, extra):
     return [
-        pltpu.VMEM((slots + EXTRA, 8, GROUP * tokens), jnp.float32),
+        pltpu.VMEM((slots + extra, 8, GROUP * tokens), jnp.float32),
         pltpu.VMEM((queries, LANES), jnp.float32),
         pltpu.VMEM((queries, LANES), jnp.int32),
         pltpu.SMEM((queries, LANES), jnp.int32),
@@ -248,48 +249,50 @@
     )
 
 
-def score_kernel(block_rows, block_count, tokens, cand_count, me, passages, blocks, out, *scratch):
+def score_kernel(block_rows, block_count, extra, tokens, cand_count, me, passages, blocks, out, *scratch):
     out[...] = score_blocks(
-        block_rows, block_count, tokens, cand_count, me[0].astype(jnp.float32), passages, blocks, *scratch
+        block_rows, block_count, extra, tokens, cand_count, me[0].astype(jnp.float32), passages, blocks, *scratch
     )
 
 
-def score(me, passages, blocks, block_rows, block_count, tokens, cand_count):
+def score(me, passages, blocks, block_rows, block_count, extra, tokens, cand_count):
     queries = block_count * (REQUEST_ROWS // 2)
     return pl.pallas_call(
-        functools.partial(score_kernel, block_rows, block_count, tokens, cand_count),
+        functools.partial(score_kernel, block_rows, block_count, extra, tokens, cand_count),
         out_shape=jax.ShapeDtypeStruct((queries, LANES), jnp.float32),
         in_specs=[pl.BlockSpec(memory_space=pltpu.SMEM), VMEM, VMEM],
         out_specs=VMEM,
-        scratch_shapes=score_scratch(passages.shape[0], tokens, queries),
+        scratch_shapes=score_scratch(passages.shape[0], tokens, queries, extra),
         compiler_params=params(16),
         cost_estimate=cost(passages, queries),
     )(me, passages, blocks)
 
 
-def last_kernel(steps, block_rows, block_count, tokens, cand_count, me, passages, blocks, line, out, *scratch):
+def last_kernel(
+    homes, block_rows, block_count, extra, tokens, cand_count, me, passages, blocks, earlier, out, *scratch
+):
     per_block = REQUEST_ROWS // 2
     result = score_blocks(
-        block_rows, block_count, tokens, cand_count, me[0].astype(jnp.float32), passages, blocks, *scratch
+        block_rows, block_count, extra, tokens, cand_count, me[0].astype(jnp.float32), passages, blocks, *scratch
     )
-    for b, step in enumerate(steps):
-        rows = slice(b * per_block, (b + 1) * per_block)
-        home = lax.rem(me[0] + (2 * len(steps) - step), 2 * len(steps))
-        out[home] = line[rows, :]
-        out[jnp.bitwise_xor(home, 1)] = result[rows, :]
-
-
-def score_last(me, passages, blocks, line, steps, block_rows, block_count, tokens, cand_count):
+    before = len(homes) - block_count
+    for b, (step, side) in enumerate(homes):
+        home = jnp.bitwise_xor(lax.rem(me[0] + (len(homes) - step), len(homes)), side)
+        at = (b if b < before else b - before) * per_block
+        out[home] = earlier[at : at + per_block, :] if b < before else result[at : at + per_block, :]
+
+
+def score_last(me, passages, blocks, earlier, homes, block_rows, block_count, extra, tokens, cand_count):
     per_block = REQUEST_ROWS // 2
     return pl.pallas_call(
-        functools.partial(last_kernel, steps, block_rows, block_count, tokens, cand_count),
-        out_shape=jax.ShapeDtypeStruct((2 * block_count, per_block, LANES), jnp.float32),
+        functools.partial(last_kernel, homes, block_rows, block_count, extra, tokens, cand_count),
+        out_shape=jax.ShapeDtypeStruct((len(homes), per_block, LANES), jnp.float32),
         in_specs=[pl.BlockSpec(memory_space=pltpu.SMEM), VMEM, VMEM, VMEM],
         out_specs=VMEM,
-        scratch_shapes=score_scratch(passages.shape[0], tokens, block_count * per_block),
+        scratch_shapes=score_scratch(passages.shape[0], tokens, block_count * per_block, extra),
         compiler_params=params(16),
         cost_estimate=cost(passages, block_count * per_block),
-    )(me, passages, blocks, line)
+    )(me, passages, blocks, earlier)
 
 
 def select_kernel(returned, owner, slot, out):
@@ -319,7 +322,7 @@
     block_rows = block.shape[0]
     filled = fill(passages, lengths, token_mask)
     me = lax.axis_index("shard").reshape(1)
-    sizes = dict(block_rows=block_rows, block_count=4, tokens=tokens, cand_count=cand_count)
+    sizes = dict(block_rows=block_rows, tokens=tokens, cand_count=cand_count)
     if shard_count == 8:
         swap = lambda x, d: lax.ppermute(x, "shard", [(i, i ^ d) for i in range(shard_count)])
         turn = lambda x, d: lax.ppermute(x, "shard", [(i, (i + d) % shard_count) for i in range(shard_count)])
@@ -329,14 +332,15 @@
         first = swap(near, 1)
         far, mid, near = lax.optimization_barrier((far, mid, near))
         second = swap(jnp.concatenate([far, mid], axis=0), 1)
-        line = jnp.concatenate([block, near, far, mid], axis=0)
-        other = jnp.concatenate([own, first, second], axis=0)
-        line_scores = score(me, filled, line, **sizes)
-        by_home = score_last(me, filled, other, line_scores, steps=(0, 6, 4, 2), **sizes)
+        early = jnp.concatenate([block, near, far, mid, own], axis=0)
+        late = jnp.concatenate([first, second], axis=0)
+        early_scores = score(me, filled, early, block_count=5, extra=24, **sizes)
+        homes = ((0, 0), (6, 0), (4, 0), (2, 0), (0, 1), (6, 1), (4, 1), (2, 1))
+        by_home = score_last(me, filled, late, early_scores, homes, block_count=3, extra=4, **sizes)
     else:
         every = lax.all_gather(block, "shard", axis=0, tiled=True)
         parts = every.reshape(shard_count // 4, 4 * block_rows, dim)
-        by_home = lax.map(lambda part: score(me, filled, part, **sizes), parts)
+        by_home = lax.map(lambda part: score(me, filled, part, block_count=4, extra=12, **sizes), parts)
         by_home = by_home.reshape(shard_count, query_count, LANES)
     returned = lax.all_to_all(by_home, "shard", split_axis=0, concat_axis=0, tiled=True)
     return select(returned, cand_owner, cand_slot)

time: 33.5 us -> 33 us (0.985)
  transfers between devices with their start and end apart: 6 -> 6, of which waited for: 1 -> 1; matrix products, arithmetic and copies ran while one was open for 0% -> 0% of each run, Pallas kernels for 20% -> 21%
where the time goes in v4:
time: 33 us; the launch traced here: 32.8 us
  Pallas kernels  12 us (36%)
  starting transfers between devices  9.76 us (30%)
  blocking collectives  9.63 us (29%)
  waiting for transfers between devices  1.19 us (4%)
    all_to_all x1, blocking collectives, local(): lax.all_to_all(by_home, 'shard', split_axis=0, concat_axis=0, tiled=True)  9.63 us
    ppermute x3, starting transfers between devices, local(): lax.ppermute(x, 'shard', [(i, (i + d) % shard_count) for i in range(shard...  6.11 us
    pallas_call x1, Pallas kernels, score(): pl.pallas_call(functools.partial(score_kernel, block_rows, block_count, e...  4.41 us
    ppermute x3, starting transfers between devices, local(): lax.ppermute(x, 'shard', [(i, i ^ d) for i in range(shard_count)])  3.65 us
    pallas_call x1, Pallas kernels, score_last(): pl.pallas_call(functools.partial(last_kernel, homes, block_rows, block_co...  3.58 us
    pallas_call x1, Pallas kernels, fill(): pl.pallas_call(fill_kernel, out_shape=pltpu.VMEM(passages.shape, jnp.bflo...  2.46 us
    ppermute x3, waiting for transfers between devices, local(): lax.ppermute(x, 'shard', [(i, (i + d) % shard_count) for i in range(shard...  1.18 us
    pallas_call x1, Pallas kernels, pack(): pl.pallas_call(pack_kernel, out_shape=pltpu.VMEM((rows.shape[0] + REQUEST...  0.86 us
  transfers between devices with their start and end apart: 6, of which 1 were waited for; matrix products, arithmetic and copies ran while one was open for 0% of the time, Pallas kernels for 21%

profile of v4, /device:TPU:0, one launch (start us, length us, event | category | flops | bytes accessed | tf_op | source)
XLA Modules:
  0.0 32.8 jit_solution(6017101340842932390)
XLA Ops:
  0.0 0.9 %shard_map.64 = bf16[272,128]{1,0:T(8,128)(2,1)S(1)} custom-call(bf16[256,128]{1,0:T(8,128)(2,1)} %bitcast.2, s32[8,100]{1,0:T(8,128)} %owner.3, s32[8,100]{1,0:T(8,128)} %slot.3), custom_call_target="tpu_custom_call" | custom-call | tf_op jit(solution)/shard_map/pallas_call | solution.py:48
  0.9 5.1 %collective-permute-start = (bf16[272,128]{1,0:T(8,128)(2,1)S(1)}, bf16[272,128]{1,0:T(8,128)(2,1)S(1)}, u32[]{:S(2)}, u32[]{:S(2)}) collective-permute-start(bf16[272,128]{1,0:T(8,128)(2,1)S(1)} %shard_map.64), channel_id=1, source_target_pairs={{0,12},{2,14},{4,0},{6,2},{8,4},{10,6},{12,8},{14,10},{1,13},{3,15... | collective-permute-start | bytes 208904 | tf_op jit(solution)/shard_map/ppermute | solution.py:328
  6.0 0.0 collective-permute-start.2
  6.0 1.0 %collective-permute-start.3 = (bf16[272,128]{1,0:T(8,128)(2,1)S(1)}, bf16[272,128]{1,0:T(8,128)(2,1)S(1)}, u32[]{:S(2)}, u32[]{:S(2)}) collective-permute-start(bf16[272,128]{1,0:T(8,128)(2,1)S(1)} %shard_map.64), channel_id=1, source_target_pairs={{0,4},{2,6},{4,8},{6,10},{8,12},{10,14},{12,0},{14,2},{1,5},{3,7},... | collective-permute-start | bytes 208904 | tf_op jit(solution)/shard_map/ppermute | solution.py:328
  7.0 1.5 %collective-permute-start.5 = (bf16[272,128]{1,0:T(8,128)(2,1)S(1)}, bf16[272,128]{1,0:T(8,128)(2,1)S(1)}, u32[]{:S(2)}, u32[]{:S(2)}) collective-permute-start(bf16[272,128]{1,0:T(8,128)(2,1)S(1)} %shard_map.64), channel_id=1, source_target_pairs={{0,2},{2,0},{4,6},{6,4},{8,10},{10,8},{12,14},{14,12},{1,3},{3,1},... | collective-permute-start | bytes 208904 | tf_op jit(solution)/shard_map/ppermute | solution.py:327
  8.5 2.5 %shard_map.65.passages = bf16[64,192,128]{2,1,0:T(8,128)(2,1)S(1)} custom-call(bf16[64,192,128]{2,1,0:T(8,128)(2,1)} %passages.1, s32[64]{0:T(128)} %lengths.1, s32[64,192]{1,0:T(8,128)} %mask.1), custom_call_target="tpu_custom_call" | custom-call | bytes 6291456 | tf_op jit(solution)/shard_map/pallas_call | solution.py:91
  11.0 0.0 collective-permute-done
  11.0 0.6 %collective-permute-start.1 = (bf16[272,128]{1,0:T(8,128)(2,1)S(1)}, bf16[272,128]{1,0:T(8,128)(2,1)S(1)}, u32[]{:S(2)}, u32[]{:S(2)}) collective-permute-start(bf16[272,128]{1,0:T(8,128)(2,1)S(1)} %collective-permute-done), channel_id=1, source_target_pairs={{0,2},{2,0},{4,6},{6,4},{8,10},{10,8},{12,14},{14,12},{1,3},{3,1},... | collective-permute-start | bytes 208904 | tf_op jit(solution)/shard_map/ppermute | solution.py:327
  11.6 1.2 %collective-permute-done.2 = bf16[272,128]{1,0:T(8,128)(2,1)S(1)} collective-permute-done((bf16[272,128]{1,0:T(8,128)(2,1)S(1)}, bf16[272,128]{1,0:T(8,128)(2,1)S(1)}, u32[]{:S(2)}, u32[]{:S(2)}) %collective-permute-start.2) | collective-permute-done | bytes 69664 | tf_op jit(solution)/shard_map/ppermute | solution.py:328
  12.8 0.0 collective-permute-done.3
  12.8 1.6 %collective-permute-start.4 = (bf16[544,128]{1,0:T(8,128)(2,1)S(1)}, bf16[544,128]{1,0:T(8,128)(2,1)S(1)}, u32[]{:S(2)}, u32[]{:S(2)}) collective-permute-start(bf16[544,128]{1,0:T(8,128)(2,1)S(1)} %pad_maximum_fusion.1), channel_id=1, source_target_pairs={{0,2},{2,0},{4,6},{6,4},{8,10},{10,8},{12,14},{14,12},{1,3},{3,1},... | collective-permute-start | bytes 417800 | tf_op jit(solution)/shard_map/ppermute | solution.py:327
  14.4 0.0 collective-permute-done.5
  14.4 4.4 %shard_map.66.earlier = f32[40,128]{1,0:T(8,128)S(1)} custom-call(s32[1]{0:T(128)} %bitcast.me, bf16[64,192,128]{2,1,0:T(8,128)(2,1)S(1)} %shard_map.65.passages, bf16[1360,128]{1,0:T(8,128)(2,1)S(1)} %constant_dynamic-update-slice_fusion.blocks), custom_call_target="tpu_custom_call" | custom-call | flops 8053063680 | bytes 3145728 | tf_op jit(solution)/shard_map/pallas_call | solution.py:260
  18.8 0.0 collective-permute-done.1
  18.8 0.0 collective-permute-done.4
  18.9 0.0 copy-start
  18.9 0.0 copy-start.1
  18.9 3.6 %shard_map.67 = f32[8,8,128]{2,1,0:T(8,128)S(1)} custom-call(s32[1]{0:T(128)} %bitcast.me, bf16[64,192,128]{2,1,0:T(8,128)(2,1)S(1)} %shard_map.65.passages, bf16[816,128]{1,0:T(8,128)(2,1)S(1)} %pad_maximum_fusion.blocks, f32[40,128]{1,0:T(8,128)S(1)} %shard_map.66.earlier), custom_call_target="tpu_custom_call" | custom-call | flops 4831838208 | bytes 3145728 | tf_op jit(solution)/shard_map/pallas_call | solution.py:287
  22.5 9.6 %all_to_all.5.returned = f32[8,8,128]{2,1,0:T(8,128)S(1)} all-to-all(f32[8,8,128]{2,1,0:T(8,128)S(1)} %shard_map.67), channel_id=1, replica_groups=mesh['groups'=2,'shard'=8,'rep'=2] {'shard'}, dimensions={0} | all-to-all | bytes 65536 | tf_op jit(solution)/shard_map/all_to_all | solution.py:345
  32.1 0.0 copy-done
  32.1 0.0 copy-done.1
  32.1 0.7 %shard_map.68 = f32[8,100]{1,0:T(8,128)} custom-call(f32[8,8,128]{2,1,0:T(8,128)S(1)} %all_to_all.5.returned, s32[8,100]{1,0:T(8,128)S(1)} %copy-done, s32[8,100]{1,0:T(8,128)S(1)} %copy-done.1), custom_call_target="tpu_custom_call" | custom-call | tf_op jit(solution)/shard_map/pallas_call | solution.py:308
  (7 shorter events, 0.1 us)
Async XLA Ops:
  0.9 10.1 %collective-permute-start = (bf16[272,128]{1,0:T(8,128)(2,1)S(1)}, bf16[272,128]{1,0:T(8,128)(2,1)S(1)}, u32[]{:S(2)}, u32[]{:S(2)}) collective-permute-start(bf16[272,128]{1,0:T(8,128)(2,1)S(1)} %shard_map.64), channel_id=1, source_target_pairs={{0,12},{2,14},{4,0},{6,2},{8,4},{10,6},{12,8},{14,10},{1,13},{3,15... | collective-permute-start | bytes 208904 | tf_op jit(solution)/shard_map/ppermute | solution.py:328
  6.0 6.8 %collective-permute-start.2 = (bf16[272,128]{1,0:T(8,128)(2,1)S(1)}, bf16[272,128]{1,0:T(8,128)(2,1)S(1)}, u32[]{:S(2)}, u32[]{:S(2)}) collective-permute-start(bf16[272,128]{1,0:T(8,128)(2,1)S(1)} %shard_map.64), channel_id=1, source_target_pairs={{0,8},{2,10},{4,12},{6,14},{8,0},{10,2},{12,4},{14,6},{1,9},{3,11}... | collective-permute-start | bytes 208904 | tf_op jit(solution)/shard_map/ppermute | solution.py:328
  6.0 6.8 %collective-permute-start.3 = (bf16[272,128]{1,0:T(8,128)(2,1)S(1)}, bf16[272,128]{1,0:T(8,128)(2,1)S(1)}, u32[]{:S(2)}, u32[]{:S(2)}) collective-permute-start(bf16[272,128]{1,0:T(8,128)(2,1)S(1)} %shard_map.64), channel_id=1, source_target_pairs={{0,4},{2,6},{4,8},{6,10},{8,12},{10,14},{12,0},{14,2},{1,5},{3,7},... | collective-permute-start | bytes 208904 | tf_op jit(solution)/shard_map/ppermute | solution.py:328
  7.0 7.4 %collective-permute-start.5 = (bf16[272,128]{1,0:T(8,128)(2,1)S(1)}, bf16[272,128]{1,0:T(8,128)(2,1)S(1)}, u32[]{:S(2)}, u32[]{:S(2)}) collective-permute-start(bf16[272,128]{1,0:T(8,128)(2,1)S(1)} %shard_map.64), channel_id=1, source_target_pairs={{0,2},{2,0},{4,6},{6,4},{8,10},{10,8},{12,14},{14,12},{1,3},{3,1},... | collective-permute-start | bytes 208904 | tf_op jit(solution)/shard_map/ppermute | solution.py:327
  11.0 7.9 %collective-permute-start.1 = (bf16[272,128]{1,0:T(8,128)(2,1)S(1)}, bf16[272,128]{1,0:T(8,128)(2,1)S(1)}, u32[]{:S(2)}, u32[]{:S(2)}) collective-permute-start(bf16[272,128]{1,0:T(8,128)(2,1)S(1)} %collective-permute-done), channel_id=1, source_target_pairs={{0,2},{2,0},{4,6},{6,4},{8,10},{10,8},{12,14},{14,12},{1,3},{3,1},... | collective-permute-start | bytes 208904 | tf_op jit(solution)/shard_map/ppermute | solution.py:327
  12.8 6.0 %collective-permute-start.4 = (bf16[544,128]{1,0:T(8,128)(2,1)S(1)}, bf16[544,128]{1,0:T(8,128)(2,1)S(1)}, u32[]{:S(2)}, u32[]{:S(2)}) collective-permute-start(bf16[544,128]{1,0:T(8,128)(2,1)S(1)} %pad_maximum_fusion.1), channel_id=1, source_target_pairs={{0,2},{2,0},{4,6},{6,4},{8,10},{10,8},{12,14},{14,12},{1,3},{3,1},... | collective-permute-start | bytes 417800 | tf_op jit(solution)/shard_map/ppermute | solution.py:327
  18.9 13.2 %copy-start = (s32[8,100]{1,0:T(8,128)S(1)}, s32[8,100]{1,0:T(8,128)}, u32[]{:S(2)}) copy-start(s32[8,100]{1,0:T(8,128)} %owner.3) | copy-start | bytes 9604
  18.9 13.2 %copy-start.1 = (s32[8,100]{1,0:T(8,128)S(1)}, s32[8,100]{1,0:T(8,128)}, u32[]{:S(2)}) copy-start(s32[8,100]{1,0:T(8,128)} %slot.3) | copy-start | bytes 9604

commit v5 on v4

--- a/solution.py
+++ b/solution.py
@@ -31,9 +31,10 @@
 def pack_kernel(rows, owner, slot, out, owner_here, slot_here, sems):
     count = rows.shape[0]
     copies = [
-        pltpu.make_async_copy(rows, out.at[pl.ds(0, count)], sems.at[0]),
+        pltpu.make_async_copy(rows.at[pl.ds(0, count // 2)], out.at[pl.ds(0, count // 2)], sems.at[0]),
         pltpu.make_async_copy(owner, owner_here, sems.at[1]),
         pltpu.make_async_copy(slot, slot_here, sems.at[2]),
+        pltpu.make_async_copy(rows.at[pl.ds(count // 2, count // 2)], out.at[pl.ds(count // 2, count // 2)], sems.at[3]),
     ]
     for copy in copies:
         copy.start()
@@ -42,6 +43,7 @@
     named = jnp.concatenate([wide(owner_here[...], -1), wide(slot_here[...], 0)], axis=0)
     out[count:, :] = named.astype(jnp.float32).astype(jnp.bfloat16)
     copies[0].wait()
+    copies[3].wait()
 
 
 def pack(rows, owner, slot):
@@ -53,7 +55,7 @@
         scratch_shapes=[
             pltpu.VMEM(owner.shape, jnp.int32),
             pltpu.VMEM(slot.shape, jnp.int32),
-            pltpu.SemaphoreType.DMA((3,)),
+            pltpu.SemaphoreType.DMA((4,)),
         ],
         compiler_params=params(4),
     )(*in_hbm(rows, owner, slot))
@@ -124,9 +126,13 @@
     number = lax.broadcasted_iota(jnp.int32, (queries, LANES), 0)
     place = lax.div(number, per_block) * block_rows + lax.rem(number, per_block) * tokens
     place = place.astype(jnp.float32)
-    lists = [jnp.sum(jnp.where(rank == r, place, 0.0), axis=0, keepdims=True) for r in range(queries)]
     count = jnp.sum(named, axis=0, keepdims=True)
-    return rank, jnp.concatenate(lists, axis=0).astype(jnp.int32), count
+    return rank, place, count
+
+
+def list_rows(rank, place, first, last):
+    rows = [jnp.sum(jnp.where(rank == r, place, 0.0), axis=0, keepdims=True) for r in range(first, last)]
+    return jnp.concatenate(rows, axis=0).astype(jnp.int32)
 
 
 def overflow_list(count, slots, most):
@@ -170,12 +176,13 @@
     slots, length, dim = passages.shape
     queries = block_count * (REQUEST_ROWS // 2)
     most = queries // GROUP
-    rank, listed, count = request_tables(blocks, me, block_rows, block_count, tokens, cand_count, slots)
+    rank, place, count = request_tables(blocks, me, block_rows, block_count, tokens, cand_count, slots)
     capacity = slots * (most - 1)
-    lists_here[...] = listed
+    lists_here[0:GROUP, :] = list_rows(rank, place, 0, GROUP)
     copies = [pltpu.make_async_copy(lists_here.at[pl.ds(0, GROUP)], lists.at[pl.ds(0, GROUP)], sems.at[0])]
     copies[0].start()
     if most > 1:
+        lists_here[GROUP:, :] = list_rows(rank, place, GROUP, queries)
         later = pl.ds(GROUP, queries - GROUP)
         copies.append(pltpu.make_async_copy(lists_here.at[later], lists.at[later], sems.at[1]))
         extras_here[0:3, 0:capacity] = overflow_list(count, slots, most)

time: 33 us -> 32.9 us (level)
  no operation moved by 1% of the time
where the time goes in v5:
time: 32.9 us; the launch traced here: 32.7 us
  Pallas kernels  11.8 us (36%)
  starting transfers between devices  9.76 us (30%)
  blocking collectives  9.72 us (30%)
  waiting for transfers between devices  1.19 us (4%)
    all_to_all x1, blocking collectives, local(): lax.all_to_all(by_home, 'shard', split_axis=0, concat_axis=0, tiled=True)  9.72 us
    ppermute x3, starting transfers between devices, local(): lax.ppermute(x, 'shard', [(i, (i + d) % shard_count) for i in range(shard...  6.11 us
    pallas_call x1, Pallas kernels, score(): pl.pallas_call(functools.partial(score_kernel, block_rows, block_count, e...  4.32 us
    ppermute x3, starting transfers between devices, local(): lax.ppermute(x, 'shard', [(i, i ^ d) for i in range(shard_count)])  3.65 us
    pallas_call x1, Pallas kernels, score_last(): pl.pallas_call(functools.partial(last_kernel, homes, block_rows, block_co...  3.54 us
    pallas_call x1, Pallas kernels, fill(): pl.pallas_call(fill_kernel, out_shape=pltpu.VMEM(passages.shape, jnp.bflo...  2.46 us
    ppermute x3, waiting for transfers between devices, local(): lax.ppermute(x, 'shard', [(i, (i + d) % shard_count) for i in range(shard...  1.18 us
    pallas_call x1, Pallas kernels, pack(): pl.pallas_call(pack_kernel, out_shape=pltpu.VMEM((rows.shape[0] + REQUEST...  0.84 us
  transfers between devices with their start and end apart: 6, of which 1 were waited for; matrix products, arithmetic and copies ran while one was open for 0% of the time, Pallas kernels for 21%

profile of v5, /device:TPU:0, one launch (start us, length us, event | category | flops | bytes accessed | tf_op | source)
XLA Modules:
  0.0 32.7 jit_solution(8068757415303729757)
XLA Ops:
  0.0 0.8 %shard_map.64 = bf16[272,128]{1,0:T(8,128)(2,1)S(1)} custom-call(bf16[256,128]{1,0:T(8,128)(2,1)} %bitcast.2, s32[8,100]{1,0:T(8,128)} %owner.3, s32[8,100]{1,0:T(8,128)} %slot.3), custom_call_target="tpu_custom_call" | custom-call | tf_op jit(solution)/shard_map/pallas_call | solution.py:50
  0.8 5.1 %collective-permute-start = (bf16[272,128]{1,0:T(8,128)(2,1)S(1)}, bf16[272,128]{1,0:T(8,128)(2,1)S(1)}, u32[]{:S(2)}, u32[]{:S(2)}) collective-permute-start(bf16[272,128]{1,0:T(8,128)(2,1)S(1)} %shard_map.64), channel_id=1, source_target_pairs={{0,12},{2,14},{4,0},{6,2},{8,4},{10,6},{12,8},{14,10},{1,13},{3,15... | collective-permute-start | bytes 208904 | tf_op jit(solution)/shard_map/ppermute | solution.py:335
  6.0 0.0 collective-permute-start.2
  6.0 1.0 %collective-permute-start.3 = (bf16[272,128]{1,0:T(8,128)(2,1)S(1)}, bf16[272,128]{1,0:T(8,128)(2,1)S(1)}, u32[]{:S(2)}, u32[]{:S(2)}) collective-permute-start(bf16[272,128]{1,0:T(8,128)(2,1)S(1)} %shard_map.64), channel_id=1, source_target_pairs={{0,4},{2,6},{4,8},{6,10},{8,12},{10,14},{12,0},{14,2},{1,5},{3,7},... | collective-permute-start | bytes 208904 | tf_op jit(solution)/shard_map/ppermute | solution.py:335
  7.0 1.5 %collective-permute-start.5 = (bf16[272,128]{1,0:T(8,128)(2,1)S(1)}, bf16[272,128]{1,0:T(8,128)(2,1)S(1)}, u32[]{:S(2)}, u32[]{:S(2)}) collective-permute-start(bf16[272,128]{1,0:T(8,128)(2,1)S(1)} %shard_map.64), channel_id=1, source_target_pairs={{0,2},{2,0},{4,6},{6,4},{8,10},{10,8},{12,14},{14,12},{1,3},{3,1},... | collective-permute-start | bytes 208904 | tf_op jit(solution)/shard_map/ppermute | solution.py:334
  8.5 2.5 %shard_map.65.passages = bf16[64,192,128]{2,1,0:T(8,128)(2,1)S(1)} custom-call(bf16[64,192,128]{2,1,0:T(8,128)(2,1)} %passages.1, s32[64]{0:T(128)} %lengths.1, s32[64,192]{1,0:T(8,128)} %mask.1), custom_call_target="tpu_custom_call" | custom-call | bytes 6291456 | tf_op jit(solution)/shard_map/pallas_call | solution.py:93
  10.9 0.0 collective-permute-done
  11.0 0.6 %collective-permute-start.1 = (bf16[272,128]{1,0:T(8,128)(2,1)S(1)}, bf16[272,128]{1,0:T(8,128)(2,1)S(1)}, u32[]{:S(2)}, u32[]{:S(2)}) collective-permute-start(bf16[272,128]{1,0:T(8,128)(2,1)S(1)} %collective-permute-done), channel_id=1, source_target_pairs={{0,2},{2,0},{4,6},{6,4},{8,10},{10,8},{12,14},{14,12},{1,3},{3,1},... | collective-permute-start | bytes 208904 | tf_op jit(solution)/shard_map/ppermute | solution.py:334
  11.6 1.2 %collective-permute-done.2 = bf16[272,128]{1,0:T(8,128)(2,1)S(1)} collective-permute-done((bf16[272,128]{1,0:T(8,128)(2,1)S(1)}, bf16[272,128]{1,0:T(8,128)(2,1)S(1)}, u32[]{:S(2)}, u32[]{:S(2)}) %collective-permute-start.2) | collective-permute-done | bytes 69664 | tf_op jit(solution)/shard_map/ppermute | solution.py:335
  12.7 0.0 collective-permute-done.3
  12.8 1.6 %collective-permute-start.4 = (bf16[544,128]{1,0:T(8,128)(2,1)S(1)}, bf16[544,128]{1,0:T(8,128)(2,1)S(1)}, u32[]{:S(2)}, u32[]{:S(2)}) collective-permute-start(bf16[544,128]{1,0:T(8,128)(2,1)S(1)} %pad_maximum_fusion.1), channel_id=1, source_target_pairs={{0,2},{2,0},{4,6},{6,4},{8,10},{10,8},{12,14},{14,12},{1,3},{3,1},... | collective-permute-start | bytes 417800 | tf_op jit(solution)/shard_map/ppermute | solution.py:334
  14.4 0.0 collective-permute-done.5
  14.4 4.3 %shard_map.66.earlier = f32[40,128]{1,0:T(8,128)S(1)} custom-call(s32[1]{0:T(128)} %bitcast.me, bf16[64,192,128]{2,1,0:T(8,128)(2,1)S(1)} %shard_map.65.passages, bf16[1360,128]{1,0:T(8,128)(2,1)S(1)} %constant_dynamic-update-slice_fusion.blocks), custom_call_target="tpu_custom_call" | custom-call | flops 8053063680 | bytes 3145728 | tf_op jit(solution)/shard_map/pallas_call | solution.py:267
  18.7 0.0 collective-permute-done.1
  18.7 0.0 collective-permute-done.4
  18.8 0.0 copy-start
  18.8 0.0 copy-start.1
  18.8 3.5 %shard_map.67 = f32[8,8,128]{2,1,0:T(8,128)S(1)} custom-call(s32[1]{0:T(128)} %bitcast.me, bf16[64,192,128]{2,1,0:T(8,128)(2,1)S(1)} %shard_map.65.passages, bf16[816,128]{1,0:T(8,128)(2,1)S(1)} %pad_maximum_fusion.blocks, f32[40,128]{1,0:T(8,128)S(1)} %shard_map.66.earlier), custom_call_target="tpu_custom_call" | custom-call | flops 4831838208 | bytes 3145728 | tf_op jit(solution)/shard_map/pallas_call | solution.py:294
  22.3 9.7 %all_to_all.5.returned = f32[8,8,128]{2,1,0:T(8,128)S(1)} all-to-all(f32[8,8,128]{2,1,0:T(8,128)S(1)} %shard_map.67), channel_id=1, replica_groups=mesh['groups'=2,'shard'=8,'rep'=2] {'shard'}, dimensions={0} | all-to-all | bytes 65536 | tf_op jit(solution)/shard_map/all_to_all | solution.py:352
  32.1 0.0 copy-done
  32.1 0.0 copy-done.1
  32.1 0.7 %shard_map.68 = f32[8,100]{1,0:T(8,128)} custom-call(f32[8,8,128]{2,1,0:T(8,128)S(1)} %all_to_all.5.returned, s32[8,100]{1,0:T(8,128)S(1)} %copy-done, s32[8,100]{1,0:T(8,128)S(1)} %copy-done.1), custom_call_target="tpu_custom_call" | custom-call | tf_op jit(solution)/shard_map/pallas_call | solution.py:315
  (7 shorter events, 0.1 us)
Async XLA Ops:
  0.8 10.1 %collective-permute-start = (bf16[272,128]{1,0:T(8,128)(2,1)S(1)}, bf16[272,128]{1,0:T(8,128)(2,1)S(1)}, u32[]{:S(2)}, u32[]{:S(2)}) collective-permute-start(bf16[272,128]{1,0:T(8,128)(2,1)S(1)} %shard_map.64), channel_id=1, source_target_pairs={{0,12},{2,14},{4,0},{6,2},{8,4},{10,6},{12,8},{14,10},{1,13},{3,15... | collective-permute-start | bytes 208904 | tf_op jit(solution)/shard_map/ppermute | solution.py:335
  6.0 6.8 %collective-permute-start.2 = (bf16[272,128]{1,0:T(8,128)(2,1)S(1)}, bf16[272,128]{1,0:T(8,128)(2,1)S(1)}, u32[]{:S(2)}, u32[]{:S(2)}) collective-permute-start(bf16[272,128]{1,0:T(8,128)(2,1)S(1)} %shard_map.64), channel_id=1, source_target_pairs={{0,8},{2,10},{4,12},{6,14},{8,0},{10,2},{12,4},{14,6},{1,9},{3,11}... | collective-permute-start | bytes 208904 | tf_op jit(solution)/shard_map/ppermute | solution.py:335
  6.0 6.8 %collective-permute-start.3 = (bf16[272,128]{1,0:T(8,128)(2,1)S(1)}, bf16[272,128]{1,0:T(8,128)(2,1)S(1)}, u32[]{:S(2)}, u32[]{:S(2)}) collective-permute-start(bf16[272,128]{1,0:T(8,128)(2,1)S(1)} %shard_map.64), channel_id=1, source_target_pairs={{0,4},{2,6},{4,8},{6,10},{8,12},{10,14},{12,0},{14,2},{1,5},{3,7},... | collective-permute-start | bytes 208904 | tf_op jit(solution)/shard_map/ppermute | solution.py:335
  7.0 7.4 %collective-permute-start.5 = (bf16[272,128]{1,0:T(8,128)(2,1)S(1)}, bf16[272,128]{1,0:T(8,128)(2,1)S(1)}, u32[]{:S(2)}, u32[]{:S(2)}) collective-permute-start(bf16[272,128]{1,0:T(8,128)(2,1)S(1)} %shard_map.64), channel_id=1, source_target_pairs={{0,2},{2,0},{4,6},{6,4},{8,10},{10,8},{12,14},{14,12},{1,3},{3,1},... | collective-permute-start | bytes 208904 | tf_op jit(solution)/shard_map/ppermute | solution.py:334
  11.0 7.8 %collective-permute-start.1 = (bf16[272,128]{1,0:T(8,128)(2,1)S(1)}, bf16[272,128]{1,0:T(8,128)(2,1)S(1)}, u32[]{:S(2)}, u32[]{:S(2)}) collective-permute-start(bf16[272,128]{1,0:T(8,128)(2,1)S(1)} %collective-permute-done), channel_id=1, source_target_pairs={{0,2},{2,0},{4,6},{6,4},{8,10},{10,8},{12,14},{14,12},{1,3},{3,1},... | collective-permute-start | bytes 208904 | tf_op jit(solution)/shard_map/ppermute | solution.py:334
  12.8 5.9 %collective-permute-start.4 = (bf16[544,128]{1,0:T(8,128)(2,1)S(1)}, bf16[544,128]{1,0:T(8,128)(2,1)S(1)}, u32[]{:S(2)}, u32[]{:S(2)}) collective-permute-start(bf16[544,128]{1,0:T(8,128)(2,1)S(1)} %pad_maximum_fusion.1), channel_id=1, source_target_pairs={{0,2},{2,0},{4,6},{6,4},{8,10},{10,8},{12,14},{14,12},{1,3},{3,1},... | collective-permute-start | bytes 417800 | tf_op jit(solution)/shard_map/ppermute | solution.py:334
  18.8 13.3 %copy-start = (s32[8,100]{1,0:T(8,128)S(1)}, s32[8,100]{1,0:T(8,128)}, u32[]{:S(2)}) copy-start(s32[8,100]{1,0:T(8,128)} %owner.3) | copy-start | bytes 9604
  18.8 13.3 %copy-start.1 = (s32[8,100]{1,0:T(8,128)S(1)}, s32[8,100]{1,0:T(8,128)}, u32[]{:S(2)}) copy-start(s32[8,100]{1,0:T(8,128)} %slot.3) | copy-start | bytes 9604

commit v6 on v4

--- a/solution.py
+++ b/solution.py
@@ -189,7 +189,7 @@
         similar = lax.dot_general(
             passages[p], jnp.concatenate(rows, axis=0), NT, preferred_element_type=jnp.float32
         )
-        return jnp.max(similar.reshape(length // 8, 8, GROUP * tokens), axis=0)
+        return jnp.max(similar, axis=0, keepdims=True)
 
     def extra_facts(e):
         live = e < extras[2, 0]
@@ -200,13 +200,13 @@
         if p == EARLY:
             for copy in copies[1:]:
                 copy.wait()
-        best[p] = group_best(p, 0)
+        best[p : p + 1, :] = group_best(p, 0)
     if most > 1:
         facts = [extra_facts(e) for e in range(extra)]
         for e, (_, p, j) in enumerate(facts):
-            best[slots + e] = group_best(p, j * GROUP)
-    table[0:GROUP, 0:slots] = token_means(jnp.max(best[0:slots], axis=1), tokens)
-    means = token_means(jnp.max(best[slots:], axis=1), tokens)
+            best[slots + e : slots + e + 1, :] = group_best(p, j * GROUP)
+    table[0:GROUP, 0:slots] = token_means(best[0:slots, :], tokens)
+    means = token_means(best[slots:, :], tokens)
     if most > 1:
         for j in range(1, most):
             total = jnp.zeros((GROUP, LANES), jnp.float32)
@@ -217,8 +217,8 @@
         def step(i, carry):
             where = [extra_facts(i * extra + u) for u in range(extra)]
             for u, (_, p, j) in enumerate(where):
-                best[u] = group_best(p, j * GROUP)
-            means = token_means(jnp.max(best[0:extra], axis=1), tokens)
+                best[u : u + 1, :] = group_best(p, j * GROUP)
+            means = token_means(best[0:extra, :], tokens)
             for u, (at, _, j) in enumerate(where):
                 rows = pl.ds(pl.multiple_of(j * GROUP, GROUP), GROUP)
                 table[rows, :] = jnp.where(lane == at, means[:, u : u + 1], table[rows, :])
@@ -233,7 +233,7 @@
 
 def score_scratch(slots, tokens, queries, extra):
     return [
-        pltpu.VMEM((slots + extra, 8, GROUP * tokens), jnp.float32),
+        pltpu.VMEM((slots + extra, GROUP * tokens), jnp.float32),
         pltpu.VMEM((queries, LANES), jnp.float32),
         pltpu.VMEM((queries, LANES), jnp.int32),
         pltpu.SMEM((queries, LANES), jnp.int32),

time: 33 us -> 33 us (level)
  no operation moved by 1% of the time
where the time goes in v6:
time: 33 us; the launch traced here: 32.8 us
  Pallas kernels  12 us (36%)
  starting transfers between devices  9.76 us (30%)
  blocking collectives  9.63 us (29%)
  waiting for transfers between devices  1.19 us (4%)
    all_to_all x1, blocking collectives, local(): lax.all_to_all(by_home, 'shard', split_axis=0, concat_axis=0, tiled=True)  9.63 us
    ppermute x3, starting transfers between devices, local(): lax.ppermute(x, 'shard', [(i, (i + d) % shard_count) for i in range(shard...  6.11 us
    pallas_call x1, Pallas kernels, score(): pl.pallas_call(functools.partial(score_kernel, block_rows, block_count, e...  4.43 us
    ppermute x3, starting transfers between devices, local(): lax.ppermute(x, 'shard', [(i, i ^ d) for i in range(shard_count)])  3.65 us
    pallas_call x1, Pallas kernels, score_last(): pl.pallas_call(functools.partial(last_kernel, homes, block_rows, block_co...  3.58 us
    pallas_call x1, Pallas kernels, fill(): pl.pallas_call(fill_kernel, out_shape=pltpu.VMEM(passages.shape, jnp.bflo...  2.46 us
    ppermute x3, waiting for transfers between devices, local(): lax.ppermute(x, 'shard', [(i, (i + d) % shard_count) for i in range(shard...  1.18 us
    pallas_call x1, Pallas kernels, pack(): pl.pallas_call(pack_kernel, out_shape=pltpu.VMEM((rows.shape[0] + REQUEST...  0.86 us
  transfers between devices with their start and end apart: 6, of which 1 were waited for; matrix products, arithmetic and copies ran while one was open for 0% of the time, Pallas kernels for 21%

profile of v6, /device:TPU:0, one launch (start us, length us, event | category | flops | bytes accessed | tf_op | source)
XLA Modules:
  0.0 32.8 jit_solution(15187943856116409629)
XLA Ops:
  0.0 0.9 %shard_map.64 = bf16[272,128]{1,0:T(8,128)(2,1)S(1)} custom-call(bf16[256,128]{1,0:T(8,128)(2,1)} %bitcast.2, s32[8,100]{1,0:T(8,128)} %owner.3, s32[8,100]{1,0:T(8,128)} %slot.3), custom_call_target="tpu_custom_call" | custom-call | tf_op jit(solution)/shard_map/pallas_call | solution.py:48
  0.9 5.1 %collective-permute-start = (bf16[272,128]{1,0:T(8,128)(2,1)S(1)}, bf16[272,128]{1,0:T(8,128)(2,1)S(1)}, u32[]{:S(2)}, u32[]{:S(2)}) collective-permute-start(bf16[272,128]{1,0:T(8,128)(2,1)S(1)} %shard_map.64), channel_id=1, source_target_pairs={{0,12},{2,14},{4,0},{6,2},{8,4},{10,6},{12,8},{14,10},{1,13},{3,15... | collective-permute-start | bytes 208904 | tf_op jit(solution)/shard_map/ppermute | solution.py:328
  6.0 0.0 collective-permute-start.2
  6.0 1.0 %collective-permute-start.3 = (bf16[272,128]{1,0:T(8,128)(2,1)S(1)}, bf16[272,128]{1,0:T(8,128)(2,1)S(1)}, u32[]{:S(2)}, u32[]{:S(2)}) collective-permute-start(bf16[272,128]{1,0:T(8,128)(2,1)S(1)} %shard_map.64), channel_id=1, source_target_pairs={{0,4},{2,6},{4,8},{6,10},{8,12},{10,14},{12,0},{14,2},{1,5},{3,7},... | collective-permute-start | bytes 208904 | tf_op jit(solution)/shard_map/ppermute | solution.py:328
  7.0 1.5 %collective-permute-start.5 = (bf16[272,128]{1,0:T(8,128)(2,1)S(1)}, bf16[272,128]{1,0:T(8,128)(2,1)S(1)}, u32[]{:S(2)}, u32[]{:S(2)}) collective-permute-start(bf16[272,128]{1,0:T(8,128)(2,1)S(1)} %shard_map.64), channel_id=1, source_target_pairs={{0,2},{2,0},{4,6},{6,4},{8,10},{10,8},{12,14},{14,12},{1,3},{3,1},... | collective-permute-start | bytes 208904 | tf_op jit(solution)/shard_map/ppermute | solution.py:327
  8.5 2.5 %shard_map.65.passages = bf16[64,192,128]{2,1,0:T(8,128)(2,1)S(1)} custom-call(bf16[64,192,128]{2,1,0:T(8,128)(2,1)} %passages.1, s32[64]{0:T(128)} %lengths.1, s32[64,192]{1,0:T(8,128)} %mask.1), custom_call_target="tpu_custom_call" | custom-call | bytes 6291456 | tf_op jit(solution)/shard_map/pallas_call | solution.py:91
  11.0 0.0 collective-permute-done
  11.0 0.6 %collective-permute-start.1 = (bf16[272,128]{1,0:T(8,128)(2,1)S(1)}, bf16[272,128]{1,0:T(8,128)(2,1)S(1)}, u32[]{:S(2)}, u32[]{:S(2)}) collective-permute-start(bf16[272,128]{1,0:T(8,128)(2,1)S(1)} %collective-permute-done), channel_id=1, source_target_pairs={{0,2},{2,0},{4,6},{6,4},{8,10},{10,8},{12,14},{14,12},{1,3},{3,1},... | collective-permute-start | bytes 208904 | tf_op jit(solution)/shard_map/ppermute | solution.py:327
  11.6 1.2 %collective-permute-done.2 = bf16[272,128]{1,0:T(8,128)(2,1)S(1)} collective-permute-done((bf16[272,128]{1,0:T(8,128)(2,1)S(1)}, bf16[272,128]{1,0:T(8,128)(2,1)S(1)}, u32[]{:S(2)}, u32[]{:S(2)}) %collective-permute-start.2) | collective-permute-done | bytes 69664 | tf_op jit(solution)/shard_map/ppermute | solution.py:328
  12.8 0.0 collective-permute-done.3
  12.8 1.6 %collective-permute-start.4 = (bf16[544,128]{1,0:T(8,128)(2,1)S(1)}, bf16[544,128]{1,0:T(8,128)(2,1)S(1)}, u32[]{:S(2)}, u32[]{:S(2)}) collective-permute-start(bf16[544,128]{1,0:T(8,128)(2,1)S(1)} %pad_maximum_fusion.1), channel_id=1, source_target_pairs={{0,2},{2,0},{4,6},{6,4},{8,10},{10,8},{12,14},{14,12},{1,3},{3,1},... | collective-permute-start | bytes 417800 | tf_op jit(solution)/shard_map/ppermute | solution.py:327
  14.4 0.0 collective-permute-done.5
  14.4 4.4 %shard_map.66.earlier = f32[40,128]{1,0:T(8,128)S(1)} custom-call(s32[1]{0:T(128)} %bitcast.me, bf16[64,192,128]{2,1,0:T(8,128)(2,1)S(1)} %shard_map.65.passages, bf16[1360,128]{1,0:T(8,128)(2,1)S(1)} %constant_dynamic-update-slice_fusion.blocks), custom_call_target="tpu_custom_call" | custom-call | flops 8053063680 | bytes 3145728 | tf_op jit(solution)/shard_map/pallas_call | solution.py:260
  18.9 0.0 collective-permute-done.1
  18.9 0.0 collective-permute-done.4
  18.9 0.0 copy-start
  18.9 0.0 copy-start.1
  18.9 3.6 %shard_map.67 = f32[8,8,128]{2,1,0:T(8,128)S(1)} custom-call(s32[1]{0:T(128)} %bitcast.me, bf16[64,192,128]{2,1,0:T(8,128)(2,1)S(1)} %shard_map.65.passages, bf16[816,128]{1,0:T(8,128)(2,1)S(1)} %pad_maximum_fusion.blocks, f32[40,128]{1,0:T(8,128)S(1)} %shard_map.66.earlier), custom_call_target="tpu_custom_call" | custom-call | flops 4831838208 | bytes 3145728 | tf_op jit(solution)/shard_map/pallas_call | solution.py:287
  22.5 9.6 %all_to_all.5.returned = f32[8,8,128]{2,1,0:T(8,128)S(1)} all-to-all(f32[8,8,128]{2,1,0:T(8,128)S(1)} %shard_map.67), channel_id=1, replica_groups=mesh['groups'=2,'shard'=8,'rep'=2] {'shard'}, dimensions={0} | all-to-all | bytes 65536 | tf_op jit(solution)/shard_map/all_to_all | solution.py:345
  32.1 0.0 copy-done
  32.1 0.0 copy-done.1
  32.1 0.7 %shard_map.68 = f32[8,100]{1,0:T(8,128)} custom-call(f32[8,8,128]{2,1,0:T(8,128)S(1)} %all_to_all.5.returned, s32[8,100]{1,0:T(8,128)S(1)} %copy-done, s32[8,100]{1,0:T(8,128)S(1)} %copy-done.1), custom_call_target="tpu_custom_call" | custom-call | tf_op jit(solution)/shard_map/pallas_call | solution.py:308
  (7 shorter events, 0.1 us)
Async XLA Ops:
  0.9 10.1 %collective-permute-start = (bf16[272,128]{1,0:T(8,128)(2,1)S(1)}, bf16[272,128]{1,0:T(8,128)(2,1)S(1)}, u32[]{:S(2)}, u32[]{:S(2)}) collective-permute-start(bf16[272,128]{1,0:T(8,128)(2,1)S(1)} %shard_map.64), channel_id=1, source_target_pairs={{0,12},{2,14},{4,0},{6,2},{8,4},{10,6},{12,8},{14,10},{1,13},{3,15... | collective-permute-start | bytes 208904 | tf_op jit(solution)/shard_map/ppermute | solution.py:328
  6.0 6.8 %collective-permute-start.2 = (bf16[272,128]{1,0:T(8,128)(2,1)S(1)}, bf16[272,128]{1,0:T(8,128)(2,1)S(1)}, u32[]{:S(2)}, u32[]{:S(2)}) collective-permute-start(bf16[272,128]{1,0:T(8,128)(2,1)S(1)} %shard_map.64), channel_id=1, source_target_pairs={{0,8},{2,10},{4,12},{6,14},{8,0},{10,2},{12,4},{14,6},{1,9},{3,11}... | collective-permute-start | bytes 208904 | tf_op jit(solution)/shard_map/ppermute | solution.py:328
  6.0 6.8 %collective-permute-start.3 = (bf16[272,128]{1,0:T(8,128)(2,1)S(1)}, bf16[272,128]{1,0:T(8,128)(2,1)S(1)}, u32[]{:S(2)}, u32[]{:S(2)}) collective-permute-start(bf16[272,128]{1,0:T(8,128)(2,1)S(1)} %shard_map.64), channel_id=1, source_target_pairs={{0,4},{2,6},{4,8},{6,10},{8,12},{10,14},{12,0},{14,2},{1,5},{3,7},... | collective-permute-start | bytes 208904 | tf_op jit(solution)/shard_map/ppermute | solution.py:328
  7.0 7.4 %collective-permute-start.5 = (bf16[272,128]{1,0:T(8,128)(2,1)S(1)}, bf16[272,128]{1,0:T(8,128)(2,1)S(1)}, u32[]{:S(2)}, u32[]{:S(2)}) collective-permute-start(bf16[272,128]{1,0:T(8,128)(2,1)S(1)} %shard_map.64), channel_id=1, source_target_pairs={{0,2},{2,0},{4,6},{6,4},{8,10},{10,8},{12,14},{14,12},{1,3},{3,1},... | collective-permute-start | bytes 208904 | tf_op jit(solution)/shard_map/ppermute | solution.py:327
  11.0 7.9 %collective-permute-start.1 = (bf16[272,128]{1,0:T(8,128)(2,1)S(1)}, bf16[272,128]{1,0:T(8,128)(2,1)S(1)}, u32[]{:S(2)}, u32[]{:S(2)}) collective-permute-start(bf16[272,128]{1,0:T(8,128)(2,1)S(1)} %collective-permute-done), channel_id=1, source_target_pairs={{0,2},{2,0},{4,6},{6,4},{8,10},{10,8},{12,14},{14,12},{1,3},{3,1},... | collective-permute-start | bytes 208904 | tf_op jit(solution)/shard_map/ppermute | solution.py:327
  12.8 6.1 %collective-permute-start.4 = (bf16[544,128]{1,0:T(8,128)(2,1)S(1)}, bf16[544,128]{1,0:T(8,128)(2,1)S(1)}, u32[]{:S(2)}, u32[]{:S(2)}) collective-permute-start(bf16[544,128]{1,0:T(8,128)(2,1)S(1)} %pad_maximum_fusion.1), channel_id=1, source_target_pairs={{0,2},{2,0},{4,6},{6,4},{8,10},{10,8},{12,14},{14,12},{1,3},{3,1},... | collective-permute-start | bytes 417800 | tf_op jit(solution)/shard_map/ppermute | solution.py:327
  18.9 13.2 %copy-start = (s32[8,100]{1,0:T(8,128)S(1)}, s32[8,100]{1,0:T(8,128)}, u32[]{:S(2)}) copy-start(s32[8,100]{1,0:T(8,128)} %owner.3) | copy-start | bytes 9604
  18.9 13.2 %copy-start.1 = (s32[8,100]{1,0:T(8,128)S(1)}, s32[8,100]{1,0:T(8,128)}, u32[]{:S(2)}) copy-start(s32[8,100]{1,0:T(8,128)} %slot.3) | copy-start | bytes 9604
